TPU v7x, 512 devices: a whole 4x4x16 slice. The times are simulated.
512 devices in a mesh: dp: 8 (over y_lo, x), ctx: 64 (over z, y_hi, core).
Axes of the slice: x: 4, y: 4 (y_hi: 2, y_lo: 2; y = y_hi * 2 + y_lo), z: 16, core: 2. Of those that a mesh axis runs over, the one named last changes fastest.
Arguments:
- queries: bfloat16 [8, 8192, 1600], P('dp', 'ctx'), may hold values from -24 to 24
- key_vectors: bfloat16 [8, 8192, 320], P('dp', 'ctx'), may hold values from -24 to 24
- value_vectors: bfloat16 [8, 8192, 320], P('dp', 'ctx'), may hold values from -6 to 6
- meta_keys: bfloat16 [128, 320], replicated, may hold values from -6 to 6
- meta_values: bfloat16 [128, 320], replicated, may hold values from -6 to 6
- windows: int32 [25], replicated, may hold values from 1 to 1024, as said below
- ssm_input: bfloat16 [8, 8192, 1600], P('dp', 'ctx'), may hold values from -6 to 6
- input_map: bfloat16 [8, 8192, 16], P('dp', 'ctx'), may hold values from -0.59765625 to 0.59765625
- output_map: bfloat16 [8, 8192, 16], P('dp', 'ctx'), may hold values from -1.5 to 1.5
- log_decay: float32 [8, 8192, 25], P('dp', 'ctx'), may hold values from -1 to 0
- cotangent: bfloat16 [8, 8192, 1600], P('dp', 'ctx'), may hold values from -6 to 6
Outputs:
- grad_queries: bfloat16 [8, 8192, 1600], P('dp', 'ctx')
- grad_keys: bfloat16 [8, 8192, 320], P('dp', 'ctx')
- grad_values: bfloat16 [8, 8192, 320], P('dp', 'ctx')
- grad_meta: float32 [2, 128, 320], P(None, 'dp', 'ctx')
- grad_input: bfloat16 [8, 8192, 1600], P('dp', 'ctx')
- grad_input_map: float32 [8, 8192, 16], P('dp', 'ctx')
- grad_output_map: float32 [8, 8192, 16], P('dp', 'ctx')
Inputs may be any that keep to these rules, and one draw needn't show every extreme that they name: `windows`: some head's look-back is exactly 1024.
All inputs are finite; a program needn't handle non-finite values.
Results may differ from a plain program's by a relative error of at most 0.011.
Values may be sent and summed in bfloat16 or wider, within the bound.
A program may use at most 128 MiB of HBM per device.

v0:
```python
import jax
import jax.numpy as jnp
from jax import lax
from jax.sharding import PartitionSpec as P

HEAD_DIM = 64
WINDOW = 1024


def from_behind(shard, axis, by):
    length = lax.axis_size(axis)
    pairs = [(i, i + by) for i in range(length) if 0 <= i + by < length]
    return lax.ppermute(shard, axis, pairs)


def entering(shard, axis, combine, identity, reverse):
    length, index = (lax.axis_size(axis), lax.axis_index(axis))
    everything = jax.tree.map(lambda part: lax.all_gather(part, axis), shard)
    start = jax.tree.map(
        lambda part, zero: jnp.broadcast_to(jnp.asarray(zero, part.dtype), part.shape),
        shard,
        identity,
    )

    def turn(k, before):
        at = length - 1 - k if reverse else k
        reached = at > index if reverse else at < index
        new = combine(before, jax.tree.map(lambda part: part[at], everything))
        return jax.tree.map(lambda a, b: jnp.where(reached, a, b), new, before)

    return lax.fori_loop(0, length, turn, start)


def ssm_prepare(b_blk, c_blk, d_blk):
    block_len = d_blk.shape[0]
    running = jnp.cumsum(d_blk, axis=0)
    block_end = running[-1]
    order_pos = jnp.arange(block_len, dtype=jnp.int32)
    causal = order_pos[:, None] >= order_pos[None, :]
    running_t = running.T
    mixing = jnp.where(causal[None], jnp.exp(running_t[:, :, None] - running_t[:, None, :]), 0.0)
    inner_prod = jnp.dot(c_blk, b_blk.T, preferred_element_type=jnp.float32)
    weights = (mixing * inner_prod[None]).astype(jnp.bfloat16)
    tail_decay = jnp.exp(block_end[None, :] - running)
    head_decay = jnp.exp(running)
    inject = (tail_decay[:, :, None] * b_blk.astype(jnp.float32)[:, None, :]).astype(jnp.bfloat16)
    readout = (head_decay[:, :, None] * c_blk.astype(jnp.float32)[:, None, :]).astype(jnp.bfloat16)
    return (running, mixing, weights, tail_decay, head_decay, inject, readout)


def carry_combine(earlier, later):
    return (earlier[0] * later[0], later[0][:, None, None] * earlier[1] + later[1])


def local(
    queries,
    key_vectors,
    value_vectors,
    meta_keys,
    meta_values,
    windows,
    ssm_input,
    input_map,
    output_map,
    log_decay,
    cotangent,
):
    head_count = windows.shape[0]
    feature_count = queries.shape[2]
    head_dim = HEAD_DIM
    kv_count = key_vectors.shape[2] // head_dim
    kv_features = key_vectors.shape[2]
    group = head_count // kv_count
    block_len = queries.shape[1]
    reach_blocks = WINDOW // block_len
    score_scale = head_dim ** (-0.5)
    position = lax.axis_index("ctx")
    own_pair = jnp.stack([key_vectors[0], value_vectors[0]])
    arrived = []
    for offset in range(1, reach_blocks + 1):
        arrived.append(from_behind(own_pair, "ctx", offset))
    window_pair = jnp.concatenate(arrived[::-1] + [own_pair], axis=1)
    key_count = window_pair.shape[1]
    query_pos = position * block_len + jnp.arange(block_len, dtype=jnp.int32)
    key_pos = (position - reach_blocks) * block_len + jnp.arange(key_count, dtype=jnp.int32)
    distance = query_pos[:, None] - key_pos[None, :]
    allowed = (distance >= 0) & (key_pos[None, :] >= 0)

    def kv_heads(matrix):
        return matrix.reshape(matrix.shape[0], kv_count, head_dim).transpose(1, 0, 2)

    def kv_tokens(tensor):
        return tensor.transpose(1, 0, 2).reshape(tensor.shape[1], kv_features)

    def query_heads(matrix):
        return matrix.reshape(matrix.shape[0], kv_count, group, head_dim).transpose(1, 2, 0, 3)

    def head_terms(head_items):
        query_h, key_h, value_h, grad_h, mkey_h, mvalue_h, window_len = head_items
        valid = allowed[None] & (distance[None] < window_len[:, None, None])
        scores = score_scale * jnp.einsum(
            "gqe,ke->gqk", query_h, key_h, preferred_element_type=jnp.float32
        )
        sink_scores = score_scale * jnp.einsum(
            "gqe,me->gqm", query_h, mkey_h, preferred_element_type=jnp.float32
        )
        row_max = jnp.maximum(
            jnp.max(jnp.where(valid, scores, -jnp.inf), axis=2), jnp.max(sink_scores, axis=2)
        )
        row_total = jnp.sum(jnp.where(valid, jnp.exp(scores - row_max[:, :, None]), 0.0), axis=2)
        row_total = row_total + jnp.sum(jnp.exp(sink_scores - row_max[:, :, None]), axis=2)
        log_total = row_max + jnp.log(row_total)
        attention = jnp.where(valid, jnp.exp(scores - log_total[:, :, None]), 0.0)
        sink_attention = jnp.exp(sink_scores - log_total[:, :, None])
        attention_half = attention.astype(jnp.bfloat16)
        sink_half = sink_attention.astype(jnp.bfloat16)
        attended = jnp.einsum(
            "gqk,ke->gqe", attention_half, value_h, preferred_element_type=jnp.float32
        )
        attended = attended + jnp.einsum(
            "gqm,me->gqe", sink_half, mvalue_h, preferred_element_type=jnp.float32
        )
        delta_row = jnp.sum(grad_h.astype(jnp.float32) * attended, axis=2)
        grad_attention = jnp.einsum(
            "gqe,ke->gqk", grad_h, value_h, preferred_element_type=jnp.float32
        )
        grad_sink = jnp.einsum("gqe,me->gqm", grad_h, mvalue_h, preferred_element_type=jnp.float32)
        dscores = (attention * (grad_attention - delta_row[:, :, None])).astype(jnp.bfloat16)
        dsink = (sink_attention * (grad_sink - delta_row[:, :, None])).astype(jnp.bfloat16)
        grad_q = jnp.einsum("gqk,ke->gqe", dscores, key_h, preferred_element_type=jnp.float32)
        grad_q = score_scale * (
            grad_q + jnp.einsum("gqm,me->gqe", dsink, mkey_h, preferred_element_type=jnp.float32)
        )
        grad_k = score_scale * jnp.einsum(
            "gqk,gqe->ke", dscores, query_h, preferred_element_type=jnp.float32
        )
        grad_v = jnp.einsum(
            "gqk,gqe->ke", attention_half, grad_h, preferred_element_type=jnp.float32
        )
        grad_mk = score_scale * jnp.einsum(
            "gqm,gqe->me", dsink, query_h, preferred_element_type=jnp.float32
        )
        grad_mv = jnp.einsum("gqm,gqe->me", sink_half, grad_h, preferred_element_type=jnp.float32)
        return (grad_q, grad_k, grad_v, grad_mk, grad_mv)

    stacked = (
        query_heads(queries[0]),
        kv_heads(window_pair[0]),
        kv_heads(window_pair[1]),
        query_heads(cotangent[0]),
        kv_heads(meta_keys),
        kv_heads(meta_values),
        windows.reshape(kv_count, group),
    )
    grad_q, grad_k, grad_v, grad_mk, grad_mv = lax.map(head_terms, stacked)
    grad_queries = (
        grad_q.transpose(2, 0, 1, 3)
        .reshape(grad_q.shape[2], feature_count)
        .astype(jnp.bfloat16)[None]
    )
    key_terms = jnp.stack([kv_tokens(grad_k), kv_tokens(grad_v)])
    own_terms = key_terms[:, reach_blocks * block_len :]
    halo_half = key_terms[:, : reach_blocks * block_len].astype(jnp.bfloat16)
    for offset in range(1, reach_blocks + 1):
        lower = (reach_blocks - offset) * block_len
        grad_piece = halo_half[:, lower : lower + block_len]
        own_terms = own_terms + from_behind(grad_piece, "ctx", -offset).astype(jnp.float32)
    grad_keys = own_terms[0].astype(jnp.bfloat16)[None]
    grad_values = own_terms[1].astype(jnp.bfloat16)[None]
    sink_terms = jnp.stack([kv_tokens(grad_mk), kv_tokens(grad_mv)])
    partial_sum = lax.psum_scatter(sink_terms, "dp", scatter_dimension=1, tiled=True)
    grad_meta = lax.psum_scatter(partial_sum, "ctx", scatter_dimension=2, tiled=True)
    ssm_heads = log_decay.shape[2]
    heads_in = ssm_input[0].reshape(block_len, ssm_heads, -1)
    grads_in = cotangent[0].reshape(block_len, ssm_heads, -1)
    b_blk = input_map[0]
    c_blk = output_map[0]
    running, mixing, weights, tail_decay, head_decay, inject, readout = ssm_prepare(
        b_blk, c_blk, log_decay[0]
    )
    block_state = jnp.einsum("lhn,lhp->hpn", inject, heads_in, preferred_element_type=jnp.float32)
    block_adjoint = jnp.einsum(
        "lhn,lhp->hpn", readout, grads_in, preferred_element_type=jnp.float32
    )
    block_decay = jnp.exp(running[-1])
    identity = (jnp.ones_like(block_decay), jnp.zeros_like(block_state))
    incoming = entering((block_decay, block_state), "ctx", carry_combine, identity, False)[1]
    adjoint = entering((block_decay, block_adjoint), "ctx", carry_combine, identity, True)[1]
    local_input = jnp.einsum("hts,thp->shp", weights, grads_in, preferred_element_type=jnp.float32)
    pair_prod = jnp.einsum("thp,shp->hts", grads_in, heads_in, preferred_element_type=jnp.float32)
    grad_gram = jnp.sum(mixing * pair_prod, axis=0).astype(jnp.bfloat16)
    input_local = jnp.dot(grad_gram.T, c_blk, preferred_element_type=jnp.float32)
    output_local = jnp.dot(grad_gram, b_blk, preferred_element_type=jnp.float32)
    heads_f = heads_in.astype(jnp.float32)
    grads_f = grads_in.astype(jnp.float32)
    carried_input = jnp.einsum(
        "lhn,hpn->lhp", inject.astype(jnp.float32), adjoint, precision=lax.Precision.HIGHEST
    )
    input_carried = jnp.sum(
        tail_decay[:, :, None]
        * jnp.einsum("lhp,hpn->lhn", heads_f, adjoint, precision=lax.Precision.HIGHEST),
        axis=1,
    )
    output_carried = jnp.sum(
        head_decay[:, :, None]
        * jnp.einsum("lhp,hpn->lhn", grads_f, incoming, precision=lax.Precision.HIGHEST),
        axis=1,
    )
    grad_input = (local_input + carried_input).reshape(block_len, -1).astype(jnp.bfloat16)[None]
    grad_input_map = (input_local + input_carried)[None]
    grad_output_map = (output_local + output_carried)[None]
    return (
        grad_queries,
        grad_keys,
        grad_values,
        grad_meta,
        grad_input,
        grad_input_map,
        grad_output_map,
    )


def solution(mesh):
    placed = (
        P("dp", "ctx", None),
        P("dp", "ctx", None),
        P("dp", "ctx", None),
        P(),
        P(),
        P(),
        P("dp", "ctx", None),
        P("dp", "ctx", None),
        P("dp", "ctx", None),
        P("dp", "ctx", None),
        P("dp", "ctx", None),
    )
    return jax.shard_map(
        local,
        mesh=mesh,
        in_specs=placed,
        out_specs=(
            P("dp", "ctx", None),
            P("dp", "ctx", None),
            P("dp", "ctx", None),
            P(None, "dp", "ctx"),
            P("dp", "ctx", None),
            P("dp", "ctx", None),
            P("dp", "ctx", None),
        ),
        check_vma=False,
    )
```

profile of v0, /device:TPU:1, one launch (start us, length us, event | category | flops | bytes accessed | tf_op | source)
XLA Modules:
  0.0 679.8 jit_solution(6452915906881641533)
XLA Ops:
  11.2 5.7 collective-permute-start
  16.9 7.0 %collective-permute-start.1 = (bf16[2,128,320]{1,2,0:T(8,128)(2,1)}, bf16[2,128,320]{1,2,0:T(8,128)(2,1)S(1)}, u32[]{:S(2)}, u32[]{:S(2)}) collective-permute-start(bf16[2,128,320]{1,2,0:T(8,128)(2,1)} %constant_dynamic-update-slice_fusion), channel_id=1, source_target_pairs={{0,7},{1,8},{2,9},{3,10},{4,11},{5,12},{6,13},{7,14},{8,15},{9,16}... | collective-permute-start | bytes 491528 | tf_op jit(solution)/shard_map/ppermute | solution.py:13
  23.8 6.2 collective-permute-start.2
  30.0 5.7 collective-permute-start.3
  35.7 3.5 collective-permute-start.4
  41.8 3.2 collective-permute-start.5
  45.0 3.3 collective-permute-start.6
  48.3 5.9 collective-permute-start.7
  54.5 2.3 collective-permute-done.7
  58.2 77.0 %while.52 = (s32[]{:T(128)}, bf16[5,5,128,64]{2,3,1,0:T(8,128)(2,1)}, f32[5,1152,64]{1,2,0:T(8,128)S(1)}, f32[5,1152,64]{1,2,0:T(8,128)}, f32[5,128,64]{1,2,0:T(...) while((s32[]{:T(128)}, ...), condition=%wide.region_6.7_spmd.clone.clone, body=%wide.region_0.6_spmd.clone.clone.sunk | while | flops 647265024 | bytes 29412212 | solution.py:155
  65.2 2.3 fusion.196
  80.6 2.3 fusion.196
  96.0 2.3 fusion.196
  111.4 2.3 fusion.196
  126.8 2.3 fusion.196
  139.7 1.6 fusion.74
  151.1 88.3 %all-gather.2 = f32[64,1,25]{2,1,0:T(1,128)S(1)} all-gather(f32[1,1,25]{2,1,0:T(1,128)S(1)} %get-tuple-element.511), channel_id=1, replica_groups=mesh['dp'=8,'ctx'=64] {'ctx'}, dimensions={0}, use_global_device_ids=true | all-gather | bytes 6500 | tf_op jit(solution)/shard_map/all_gather | solution.py:18
  243.3 2.1 collective-permute-start.8
  247.7 1.9 collective-permute-done.13
  249.6 15.2 %collective-permute-done.14 = bf16[2,128,320]{1,2,0:T(8,128)(2,1)S(1)} collective-permute-done((bf16[2,128,320]{1,2,0:T(8,128)(2,1)}, bf16[2,128,320]{1,2,0:T(8,128)(2,1)S(1)}, u32[]{:S(2)}, u32[]{:S(2)}) %collective-permute-start.14) | collective-permute-done | bytes 163872 | tf_op jit(solution)/shard_map/ppermute | solution.py:13
  264.8 4.1 collective-permute-done.15
  271.6 255.2 %all-reduce.1 = f32[2,16,320]{1,0,2:T(2,128)S(1)} all-reduce(f32[2,16,320]{1,0,2:T(2,128)S(1)} %copy.47), channel_id=5, replica_groups=mesh['dp'=8,'ctx'=64] {'ctx'}, use_global_device_ids=true, to_apply=%region_8.9.clone | all-reduce | flops 10240 | bytes 81920
  527.5 70.6 %while.50 = (s32[]{:T(128)}, f32[25,64,16]{1,2,0:T(8,128)S(1)}, s32[]{:T(128)}, f32[64,25]{1,0:T(8,128)S(1)}, f32[64,25,64,16]{2,3,1,0:T(8,128)}, /*index=5*/s32[]{:T(128)}, s32[]{:T(128)}, s32[]{:T(128)}, s32[]{:T(128)}) while((s32[]{:T(128)}, f32[25,64,16]{1,2,0:T(8,128)S(1)}, s32[]{:T(128)}, f32[64,25]{1,0:T(8,128)S(1)}, ...), condition=%wide.region_11.12_spmd.clone, body=%wide.region_10.11_spmd.clone.sunk | while | flops 102408 | bytes 307667 | solution.py:31
  599.4 69.6 %while.51 = (s32[]{:T(128)}, f32[25,64,16]{1,2,0:T(8,128)S(1)}, s32[]{:T(128)}, f32[64,25]{1,0:T(8,128)S(1)}, f32[64,25,64,16]{2,3,1,0:T(8,128)}, /*index=5*/s32[]{:T(128)}, s32[]{:T(128)}) while((s32[]{:T(128)}, f32[25,64,16]{1,2,0:T(8,128)S(1)}, s32[]{:T(128)}, f32[64,25]{1,0:T(8,128)S(1)}, f32[64,25,64,16]{2,3,1,0:T(8,128)}, ...), condition=%wide.region_15.16_spmd.clone, body=%wide.region_14.15_spmd.clone.sunk | while | flops 102404 | bytes 307605 | solution.py:31
  (455 shorter events, 234.5 us)
Async XLA Ops:
  8.0 130.6 %copy-start = (bf16[1,128,1600]{1,2,0:T(8,128)(2,1)S(1)}, bf16[1,128,1600]{1,2,0:T(8,128)(2,1)}, u32[]{:S(2)}) copy-start(bf16[1,128,1600]{1,2,0:T(8,128)(2,1)} %param.23) | copy-start | bytes 1228804
  8.0 262.6 %all-reduce.4.cloned.1.call-start = ((), (), s32[]{:S(2)}) async-start(), calls=%async_computation.2 | async-start | bytes 786432
  11.2 30.6 %collective-permute-start = (bf16[2,128,320]{1,2,0:T(8,128)(2,1)}, bf16[2,128,320]{1,2,0:T(8,128)(2,1)S(1)}, u32[]{:S(2)}, u32[]{:S(2)}) collective-permute-start(bf16[2,128,320]{1,2,0:T(8,128)(2,1)} %constant_dynamic-update-slice_fusion), channel_id=1, source_target_pairs={{0,8},{1,9},{2,10},{3,11},{4,12},{5,13},{6,14},{7,15},{8,16},{9,17... | collective-permute-start | bytes 491528 | tf_op jit(solution)/shard_map/ppermute | solution.py:13
  16.9 28.1 %collective-permute-start.1 = (bf16[2,128,320]{1,2,0:T(8,128)(2,1)}, bf16[2,128,320]{1,2,0:T(8,128)(2,1)S(1)}, u32[]{:S(2)}, u32[]{:S(2)}) collective-permute-start(bf16[2,128,320]{1,2,0:T(8,128)(2,1)} %constant_dynamic-update-slice_fusion), channel_id=1, source_target_pairs={{0,7},{1,8},{2,9},{3,10},{4,11},{5,12},{6,13},{7,14},{8,15},{9,16}... | collective-permute-start | bytes 491528 | tf_op jit(solution)/shard_map/ppermute | solution.py:13
  23.8 24.5 %collective-permute-start.2 = (bf16[2,128,320]{1,2,0:T(8,128)(2,1)}, bf16[2,128,320]{1,2,0:T(8,128)(2,1)S(1)}, u32[]{:S(2)}, u32[]{:S(2)}) collective-permute-start(bf16[2,128,320]{1,2,0:T(8,128)(2,1)} %constant_dynamic-update-slice_fusion), channel_id=1, source_target_pairs={{0,6},{1,7},{2,8},{3,9},{4,10},{5,11},{6,12},{7,13},{8,14},{9,15},... | collective-permute-start | bytes 491528 | tf_op jit(solution)/shard_map/ppermute | solution.py:13
  30.0 24.2 %collective-permute-start.3 = (bf16[2,128,320]{1,2,0:T(8,128)(2,1)}, bf16[2,128,320]{1,2,0:T(8,128)(2,1)S(1)}, u32[]{:S(2)}, u32[]{:S(2)}) collective-permute-start(bf16[2,128,320]{1,2,0:T(8,128)(2,1)} %constant_dynamic-update-slice_fusion), channel_id=1, source_target_pairs={{0,5},{1,6},{2,7},{3,8},{4,9},{5,10},{6,11},{7,12},{8,13},{9,14},{... | collective-permute-start | bytes 491528 | tf_op jit(solution)/shard_map/ppermute | solution.py:13
  35.7 18.6 %collective-permute-start.4 = (bf16[2,128,320]{1,2,0:T(8,128)(2,1)}, bf16[2,128,320]{1,2,0:T(8,128)(2,1)S(1)}, u32[]{:S(2)}, u32[]{:S(2)}) collective-permute-start(bf16[2,128,320]{1,2,0:T(8,128)(2,1)} %constant_dynamic-update-slice_fusion), channel_id=1, source_target_pairs={{0,4},{1,5},{2,6},{3,7},{4,8},{5,9},{6,10},{7,11},{8,12},{9,13},{1... | collective-permute-start | bytes 491528 | tf_op jit(solution)/shard_map/ppermute | solution.py:13
  40.1 16.7 %copy-start.4 = (bf16[1,128,320]{1,2,0:T(8,128)(2,1)S(1)}, bf16[1,128,320]{1,2,0:T(8,128)(2,1)}, u32[]{:S(2)}) copy-start(bf16[1,128,320]{1,2,0:T(8,128)(2,1)} %param.18) | copy-start | bytes 245764
  40.3 16.6 %copy-start.5 = (bf16[1,128,320]{1,2,0:T(8,128)(2,1)S(1)}, bf16[1,128,320]{1,2,0:T(8,128)(2,1)}, u32[]{:S(2)}) copy-start(bf16[1,128,320]{1,2,0:T(8,128)(2,1)} %param.19) | copy-start | bytes 245764
  41.8 12.6 %collective-permute-start.5 = (bf16[2,128,320]{1,2,0:T(8,128)(2,1)}, bf16[2,128,320]{1,2,0:T(8,128)(2,1)S(1)}, u32[]{:S(2)}, u32[]{:S(2)}) collective-permute-start(bf16[2,128,320]{1,2,0:T(8,128)(2,1)} %constant_dynamic-update-slice_fusion), channel_id=1, source_target_pairs={{0,3},{1,4},{2,5},{3,6},{4,7},{5,8},{6,9},{7,10},{8,11},{9,12},{10... | collective-permute-start | bytes 491528 | tf_op jit(solution)/shard_map/ppermute | solution.py:13
  45.0 9.4 %collective-permute-start.6 = (bf16[2,128,320]{1,2,0:T(8,128)(2,1)}, bf16[2,128,320]{1,2,0:T(8,128)(2,1)S(1)}, u32[]{:S(2)}, u32[]{:S(2)}) collective-permute-start(bf16[2,128,320]{1,2,0:T(8,128)(2,1)} %constant_dynamic-update-slice_fusion), channel_id=1, source_target_pairs={{0,2},{1,3},{2,4},{3,5},{4,6},{5,7},{6,8},{7,9},{8,10},{9,11},{10,... | collective-permute-start | bytes 491528 | tf_op jit(solution)/shard_map/ppermute | solution.py:13
  48.3 8.4 %collective-permute-start.7 = (bf16[2,128,320]{1,2,0:T(8,128)(2,1)}, bf16[2,128,320]{1,2,0:T(8,128)(2,1)S(1)}, u32[]{:S(2)}, u32[]{:S(2)}) collective-permute-start(bf16[2,128,320]{1,2,0:T(8,128)(2,1)} %constant_dynamic-update-slice_fusion), channel_id=1, source_target_pairs={{0,1},{1,2},{2,3},{3,4},{4,5},{5,6},{6,7},{7,8},{8,9},{9,10},{10,1... | collective-permute-start | bytes 491528 | tf_op jit(solution)/shard_map/ppermute | solution.py:13
  137.3 390.2 %all-gather.6.cloned.1.call-start = ((), (), s32[]{:S(2)}) async-start(), calls=%async_computation | async-start | bytes 13312000 | tf_op jit(solution)/shard_map/all_gather | solution.py:18
  138.5 460.9 %all-gather.8.cloned.1.call-start = ((), (), s32[]{:S(2)}) async-start(), calls=%async_computation.1 | async-start | bytes 13312000 | tf_op jit(solution)/shard_map/all_gather | solution.py:18
  142.5 99.5 %collective-permute-start.10 = (bf16[2,128,320]{1,2,0:T(8,128)(2,1)}, bf16[2,128,320]{1,2,0:T(8,128)(2,1)S(1)}, u32[]{:S(2)}, u32[]{:S(2)}) collective-permute-start(bf16[2,128,320]{1,2,0:T(8,128)(2,1)} %get-tuple-element.502), channel_id=1, source_target_pairs={{3,0},{4,1},{5,2},{6,3},{7,4},{8,5},{9,6},{10,7},{11,8},{12,9},{13... | collective-permute-start | bytes 491528 | tf_op jit(solution)/shard_map/ppermute | solution.py:13
  143.8 99.6 %collective-permute-start.11 = (bf16[2,128,320]{1,2,0:T(8,128)(2,1)}, bf16[2,128,320]{1,2,0:T(8,128)(2,1)S(1)}, u32[]{:S(2)}, u32[]{:S(2)}) collective-permute-start(bf16[2,128,320]{1,2,0:T(8,128)(2,1)} %get-tuple-element.501), channel_id=1, source_target_pairs={{4,0},{5,1},{6,2},{7,3},{8,4},{9,5},{10,6},{11,7},{12,8},{13,9},{1... | collective-permute-start | bytes 491528 | tf_op jit(solution)/shard_map/ppermute | solution.py:13
  145.1 100.4 %collective-permute-start.12 = (bf16[2,128,320]{1,2,0:T(8,128)(2,1)}, bf16[2,128,320]{1,2,0:T(8,128)(2,1)}, u32[]{:S(2)}, u32[]{:S(2)}) collective-permute-start(bf16[2,128,320]{1,2,0:T(8,128)(2,1)} %get-tuple-element.500), channel_id=1, source_target_pairs={{5,0},{6,1},{7,2},{8,3},{9,4},{10,5},{11,6},{12,7},{13,8},{14,9},{... | collective-permute-start | bytes 491528 | tf_op jit(solution)/shard_map/ppermute | solution.py:13
  239.4 10.2 %collective-permute-start.13 = (bf16[2,128,320]{1,2,0:T(8,128)(2,1)}, bf16[2,128,320]{1,2,0:T(8,128)(2,1)S(1)}, u32[]{:S(2)}, u32[]{:S(2)}) collective-permute-start(bf16[2,128,320]{1,2,0:T(8,128)(2,1)} %get-tuple-element.499), channel_id=1, source_target_pairs={{6,0},{7,1},{8,2},{9,3},{10,4},{11,5},{12,6},{13,7},{14,8},{15,9},... | collective-permute-start | bytes 491528 | tf_op jit(solution)/shard_map/ppermute | solution.py:13
  240.7 24.1 %collective-permute-start.14 = (bf16[2,128,320]{1,2,0:T(8,128)(2,1)}, bf16[2,128,320]{1,2,0:T(8,128)(2,1)S(1)}, u32[]{:S(2)}, u32[]{:S(2)}) collective-permute-start(bf16[2,128,320]{1,2,0:T(8,128)(2,1)} %get-tuple-element.498), channel_id=1, source_target_pairs={{7,0},{8,1},{9,2},{10,3},{11,4},{12,5},{13,6},{14,7},{15,8},{16,9}... | collective-permute-start | bytes 491528 | tf_op jit(solution)/shard_map/ppermute | solution.py:13
  242.0 26.8 %collective-permute-start.15 = (bf16[2,128,320]{1,2,0:T(8,128)(2,1)}, bf16[2,128,320]{1,2,0:T(8,128)(2,1)S(1)}, u32[]{:S(2)}, u32[]{:S(2)}) collective-permute-start(bf16[2,128,320]{1,2,0:T(8,128)(2,1)} %get-tuple-element.497), channel_id=1, source_target_pairs={{8,0},{9,1},{10,2},{11,3},{12,4},{13,5},{14,6},{15,7},{16,8},{17,9... | collective-permute-start | bytes 491528 | tf_op jit(solution)/shard_map/ppermute | solution.py:13
  243.3 25.5 %collective-permute-start.8 = (bf16[2,128,320]{1,2,0:T(8,128)(2,1)S(1)}, bf16[2,128,320]{1,2,0:T(8,128)(2,1)S(1)}, u32[]{:S(2)}, u32[]{:S(2)}) collective-permute-start(bf16[2,128,320]{1,2,0:T(8,128)(2,1)S(1)} %get-tuple-element.496), channel_id=1, source_target_pairs={{1,0},{2,1},{3,2},{4,3},{5,4},{6,5},{7,6},{8,7},{9,8},{10,9},{11,1... | collective-permute-start | bytes 491528 | tf_op jit(solution)/shard_map/ppermute | solution.py:13
  245.5 23.4 %copy-start.3 = (f32[5,1152,64]{1,2,0:T(8,128)S(1)}, f32[5,1152,64]{1,2,0:T(8,128)}, u32[]{:S(2)}) copy-start(f32[5,1152,64]{1,2,0:T(8,128)} %get-tuple-element.316) | copy-start | bytes 4423684
  245.5 23.4 %collective-permute-start.9 = (bf16[2,128,320]{1,2,0:T(8,128)(2,1)S(1)}, bf16[2,128,320]{1,2,0:T(8,128)(2,1)S(1)}, u32[]{:S(2)}, u32[]{:S(2)}) collective-permute-start(bf16[2,128,320]{1,2,0:T(8,128)(2,1)S(1)} %get-tuple-element.503), channel_id=1, source_target_pairs={{2,0},{3,1},{4,2},{5,3},{6,4},{7,5},{8,6},{9,7},{10,8},{11,9},{12,... | collective-permute-start | bytes 491528 | tf_op jit(solution)/shard_map/ppermute | solution.py:13
  599.4 71.5 %copy-start.8 = (f32[128,128]{1,0:T(8,128)S(1)}, f32[128,128]{1,0:T(8,128)}, u32[]{:S(2)}) copy-start(f32[128,128]{1,0:T(8,128)} %fusion.107) | copy-start | bytes 196612
  (6 other events, 13.1 us)
Sparse Core Ops, SparseCore 0:
  137.4 90.1 all-reduce.3
Sparse Core Ops, SparseCore 1:
  141.6 199.4 all-gather.5
  344.7 179.2 all-gather.7
where the time goes:
time: 690 us; the launch traced here: 680 us
  blocking collectives  344 us (50%)
  other arithmetic  150 us (22%)
  matrix products  73.1 us (11%)
  starting transfers between devices  51.8 us (8%)
  waiting for transfers between devices  23.5 us (3%)
  between operations  17.3 us (3%)
  local copies, waits for them, and re-layouts  14.7 us (2%)
    unnamed x1, blocking collectives  255 us
    select_n x128, other arithmetic, turn(): return jax.tree.map(lambda a, b: jnp.where(reached, a, b), new, before)  134 us
    all_gather x1, blocking collectives, entering(): everything = jax.tree.map(lambda part: lax.all_gather(part, axis), shard)  88.3 us
    ppermute x16, starting transfers between devices, from_behind(): return lax.ppermute(shard, axis, pairs)  51.7 us
    ppermute x16, waiting for transfers between devices, from_behind(): return lax.ppermute(shard, axis, pairs)  23.5 us
  transfers between devices with their start and end apart: 19, of which 4 were waited for; matrix products, arithmetic and copies ran while one was open for 12% of the time, Pallas kernels for 0%

commit v1 on v0

v1 whole, which is shorter than its diff:
```python
import functools

import jax
import jax.numpy as jnp
from jax import lax
from jax.experimental import pallas as pl
from jax.experimental.pallas import tpu as pltpu
from jax.sharding import PartitionSpec as P

BF = jnp.bfloat16
F32 = jnp.float32
MESH = pl.DeviceIdType.MESH
HEADS, KVH, GROUP, HD = 25, 5, 5, 64
TOK, WIDTH, KVW, STATE = 128, 1600, 320, 16
QL = 448
NT = (((1,), (1,)), ((), ()))
TN = (((0,), (0,)), ((), ()))


def dot(a, b, dims=(((1,), (0,)), ((), ()))):
    return lax.dot_general(a, b, dims, preferred_element_type=F32)


def split3(v):
    hi = v.astype(BF)
    rest = v - hi.astype(F32)
    mid = rest.astype(BF)
    low = (rest - mid.astype(F32)).astype(BF)
    return hi, mid, low


def dot3(v, onehot):
    hi, mid, low = split3(v)
    return dot(hi, onehot) + dot(mid, onehot) + dot(low, onehot)


def iota(shape, dim):
    return lax.broadcasted_iota(jnp.int32, shape, dim)


def places():
    dp, i = lax.axis_index("dp"), lax.axis_index("ctx")
    return dp, i, i % 2, (i // 2) % 2, i // 4


def ctx_kernel(
    key, val, x, g, bm, cm, ld,
    win, gin, gbm, gcm,
    own, xt, gt, texp, loc, stq, r1, d0, d1, s2, r2, d2s, d2, s3, r3, d3s, d3, ib, ob, inc, adj,
    own_sem, kv_send, kv_recv, c_send, c_recv, q1_send, q1_recv, q2_send, q2_recv, q3_send, q3_recv, q4_send, q4_recv,
):
    dp, i, core, yh, z = places()
    c = i % 4
    zl, zh = z % 4, z // 4
    up = ((z + 1) % 16) * 4 + c
    down = ((z + 15) % 16) * 4 + c
    base = i - c
    group = [base + (c + k) % 4 for k in (1, 2, 3)]
    near = [(zh * 4 + (zl + k) % 4) * 4 + c for k in (1, 2, 3)]
    far = [(((zh + k) % 4) * 4 + zl) * 4 + c for k in (1, 2, 3)]
    mate = base + (c + 1 - 2 * core)
    across = base + (c + 2) % 4

    barrier = pltpu.get_barrier_semaphore()
    for to in group + near + far + [down]:
        pl.semaphore_signal(barrier, inc=1, device_id=(dp, to), device_id_type=MESH)

    for k in range(KVH):
        own[k, :, 0:HD] = key[:, HD * k : HD * k + HD]
        own[k, :, HD : 2 * HD] = val[:, HD * k : HD * k + HD]
    pl.semaphore_wait(barrier, 10)

    def kv_copy(src, dst_slot, n, to):
        return pltpu.make_async_remote_copy(
            src_ref=src, dst_ref=win.at[dst_slot], send_sem=kv_send.at[n], recv_sem=kv_recv.at[n],
            device_id=(dp, to), device_id_type=MESH,
        )

    def mate_copy(src, d, n):
        there = (d + core * 9 + (1 - core)) % 10
        return pltpu.make_async_remote_copy(
            src_ref=src, dst_ref=win.at[there], send_sem=c_send.at[n], recv_sem=c_recv.at[n],
            device_id=(dp, mate), device_id_type=MESH,
        )

    keep = pltpu.make_async_copy(own, win.at[0], own_sem)
    step_a = kv_copy(own, 4, 0, up)
    step_y0 = kv_copy(own, 2, 1, across)
    step_y1 = kv_copy(win.at[4], 2, 1, across)
    step_b = kv_copy(win.at[2], 6, 2, up)
    step_c = kv_copy(win.at[4], 8, 3, up)
    mates = [mate_copy(own, 0, 0)] + [mate_copy(win.at[d], d, n + 1) for n, d in enumerate((4, 2, 8, 6))]
    step_a.start()

    @pl.when(yh == 0)
    def _():
        step_y0.start()

    keep.start()
    mates[0].start()

    rows, cols = iota((TOK, TOK), 0), iota((TOK, TOK), 1)
    tri = (rows >= cols).astype(BF)
    run = jnp.zeros((TOK, TOK), F32)
    ldv = jnp.concatenate([ld[...], jnp.zeros((TOK, TOK - HEADS), F32)], axis=1)
    for part in split3(ldv):
        run = run + dot(tri, part)
    run_t = run.T
    end = run[TOK - 1 : TOK, :]
    spread = (iota((32, WIDTH), 0) == iota((32, WIDTH), 1) // HD).astype(BF)
    tail_x = dot(jnp.exp(end - run)[:, :32].astype(BF), spread)
    texp[...] = tail_x
    xt[...] = (tail_x * x[...].astype(F32)).astype(BF)
    gt[...] = (dot(jnp.exp(run)[:, :32].astype(BF), spread) * g[...].astype(F32)).astype(BF)
    for w, terms in enumerate((dot(bm[...], xt[...], TN), dot(cm[...], gt[...], TN))):
        for q in range(4):
            n = min(QL, WIDTH - QL * q)
            stq[q, w] = jnp.concatenate(
                [terms[:, QL * q : QL * q + n], jnp.zeros((STATE, 512 - n), F32)], axis=1
            ).astype(BF)
    d0[...] = jnp.exp(jnp.broadcast_to(end, (8, TOK)))

    def pair(src, dst, send, recv, n, to):
        return pltpu.make_async_remote_copy(
            src_ref=src, dst_ref=dst, send_sem=send.at[n], recv_sem=recv.at[n],
            device_id=(dp, to), device_id_type=MESH,
        )

    q1 = []
    for n, k in enumerate((1, 2, 3)):
        q1.append(pair(stq.at[(c + k) % 4], r1.at[c], q1_send, q1_recv, n, group[n]))
        q1.append(pair(d0, d1.at[c], q1_send, q1_recv, 3 + n, group[n]))
    for copy in q1:
        copy.start()
    r1[c] = stq[c]
    d1[c] = d0[...]

    step_a.wait_recv()
    step_c.start()

    @pl.when(yh == 1)
    def _():
        step_y1.start()

    mates[1].start()

    row, lane = iota((32, 512), 0), iota((32, 512), 1)
    onehot = ((row == 7 * c + lane // HD) & (lane < QL)).astype(BF)

    def expand(d):
        wide = dot3(d[...].reshape(32, TOK)[:, :32], onehot)
        return [jnp.broadcast_to(wide[8 * j : 8 * j + 1], (STATE, 512)) for j in range(4)]

    for copy in q1:
        copy.wait_recv()
    dec1 = expand(d1)
    st1 = [r1[j, 0].astype(F32) for j in range(4)]
    ad1 = [r1[j, 1].astype(F32) for j in range(4)]
    total = st1[0]
    back = ad1[3]
    for j in range(1, 4):
        total = dec1[j] * total + st1[j]
        back = dec1[3 - j] * back + ad1[3 - j]
    s2[0] = total.astype(BF)
    s2[1] = back.astype(BF)
    d2s[...] = d1[0] * d1[1] * d1[2] * d1[3]
    q2 = []
    for n in range(3):
        q2.append(pair(s2, r2.at[zl], q2_send, q2_recv, n, near[n]))
        q2.append(pair(d2s, d2.at[zl], q2_send, q2_recv, 3 + n, near[n]))
    for copy in q2:
        copy.start()
    r2[zl] = s2[...]
    d2[zl] = d2s[...]

    inner_t = dot(bm[...], cm[...], NT)
    gram_t = jnp.zeros((TOK, TOK), F32)

    def local_head(h, gram_t):
        xh, gh = x[:, HD * h : HD * h + HD], g[:, HD * h : HD * h + HD]
        diff = run_t[h : h + 1, :] - run[:, h : h + 1]
        mix = jnp.where(cols >= rows, jnp.exp(diff), 0.0)
        loc[:, HD * h : HD * h + HD] = dot((mix * inner_t).astype(BF), gh)
        return gram_t + mix * dot(xh, gh, NT)

    for h in range(0, 13):
        gram_t = local_head(h, gram_t)

    step_y1.wait_recv()
    step_b.start()
    mates[2].start()

    for copy in q2:
        copy.wait_recv()
    dec2 = expand(d2)
    st2 = [r2[j, 0].astype(F32) for j in range(4)]
    ad2 = [r2[j, 1].astype(F32) for j in range(4)]
    total = st2[0]
    back = ad2[3]
    for j in range(1, 4):
        total = dec2[j] * total + st2[j]
        back = dec2[3 - j] * back + ad2[3 - j]
    s3[0] = total.astype(BF)
    s3[1] = back.astype(BF)
    d3s[...] = d2[0] * d2[1] * d2[2] * d2[3]
    q3 = []
    for n, k in enumerate((1, 2, 3)):
        there = (zh + k) % 4
        which = jnp.where(there > zh, 0, 1)
        q3.append(pair(s3.at[which], r3.at[zh], q3_send, q3_recv, n, far[n]))
        q3.append(pair(d3s, d3.at[zh], q3_send, q3_recv, 3 + n, far[n]))
    for copy in q3:
        copy.start()
    r3[zh] = s3[0]
    d3[zh] = d3s[...]

    for h in range(13, HEADS):
        gram_t = local_head(h, gram_t)
    gram_t = gram_t.astype(BF)
    in_local = dot(gram_t, cm[...])
    out_local = dot(gram_t, bm[...], TN)

    step_c.wait_recv()
    mates[3].start()
    step_b.wait_recv()
    mates[4].start()

    for copy in q3:
        copy.wait_recv()
    dec3 = expand(d3)
    zero = jnp.zeros((STATE, 512), F32)
    ahead, behind = zero, zero
    for j in range(4):
        ahead = jnp.where(j < zh, dec3[j] * ahead + r3[j].astype(F32), ahead)
        b = 3 - j
        behind = jnp.where(b > zh, dec3[b] * behind + r3[b].astype(F32), behind)
    for j in range(4):
        ahead = jnp.where(j < zl, dec2[j] * ahead + st2[j], ahead)
        b = 3 - j
        behind = jnp.where(b > zl, dec2[b] * behind + ad2[b], behind)
    for j in range(4):
        ib[j, 0] = ahead.astype(BF)
        ahead = dec1[j] * ahead + st1[j]
        b = 3 - j
        ib[b, 1] = behind.astype(BF)
        behind = dec1[b] * behind + ad1[b]
    q4 = [
        pair(ib.at[(c + k) % 4], ob.at[c], q4_send, q4_recv, n, group[n]) for n, k in enumerate((1, 2, 3))
    ]
    for copy in q4:
        copy.start()
    ob[c] = ib[c]
    for copy in q4:
        copy.wait_recv()
    for q in range(4):
        n = min(QL, WIDTH - QL * q)
        inc[:, QL * q : QL * q + n] = ob[q, 0].astype(F32)[:, :n]
        adj[:, QL * q : QL * q + n] = ob[q, 1].astype(F32)[:, :n]
    inc_h, adj_h = inc[...].astype(BF), adj[...].astype(BF)
    gin[...] = (loc[...] + texp[...] * dot(bm[...], adj_h)).astype(BF)
    gbm[...] = in_local + dot(xt[...], adj_h, NT)
    gcm[...] = out_local + dot(gt[...], inc_h, NT)

    keep.wait()
    for copy in mates:
        copy.wait_recv()
        copy.wait_send()
    for copy in [step_a, step_y1, step_b, step_c] + q1 + q2 + q3 + q4:
        copy.wait_send()


def run_ctx(key, val, x, g, bm, cm, ld):
    dma = pltpu.SemaphoreType.DMA
    vm = pltpu.VMEM
    return pl.pallas_call(
        ctx_kernel,
        out_shape=(
            jax.ShapeDtypeStruct((10, KVH, TOK, TOK), BF),
            jax.ShapeDtypeStruct((TOK, WIDTH), BF),
            jax.ShapeDtypeStruct((TOK, STATE), F32),
            jax.ShapeDtypeStruct((TOK, STATE), F32),
        ),
        in_specs=[pl.BlockSpec(memory_space=vm)] * 7,
        out_specs=(pl.BlockSpec(memory_space=pl.ANY),) + (pl.BlockSpec(memory_space=vm),) * 3,
        scratch_shapes=[
            vm((KVH, TOK, TOK), BF),
            vm((TOK, WIDTH), BF),
            vm((TOK, WIDTH), BF),
            vm((TOK, WIDTH), F32),
            vm((TOK, WIDTH), F32),
            vm((4, 2, STATE, 512), BF),
            vm((4, 2, STATE, 512), BF),
            vm((8, TOK), F32),
            vm((4, 8, TOK), F32),
            vm((2, STATE, 512), BF),
            vm((4, 2, STATE, 512), BF),
            vm((8, TOK), F32),
            vm((4, 8, TOK), F32),
            vm((2, STATE, 512), BF),
            vm((4, STATE, 512), BF),
            vm((8, TOK), F32),
            vm((4, 8, TOK), F32),
            vm((4, 2, STATE, 512), BF),
            vm((4, 2, STATE, 512), BF),
            vm((STATE, WIDTH), F32),
            vm((STATE, WIDTH), F32),
            dma,
            dma((4,)), dma((4,)), dma((5,)), dma((5,)),
            dma((6,)), dma((6,)), dma((6,)), dma((6,)), dma((6,)), dma((6,)), dma((3,)), dma((3,)),
        ],
        compiler_params=pltpu.CompilerParams(
            collective_id=0, has_side_effects=True, vmem_limit_bytes=40 * 1024 * 1024
        ),
        name="halo_and_scan",
    )(key, val, x, g, bm, cm, ld)


def attention_kernel(wins, qs, gs, win, mk, mv, gq, pieces, own, sink, qg, metas, dist, ps, dqs):
    i = lax.axis_index("ctx")
    zeros = jnp.zeros((TOK, HD), BF)
    for k in range(KVH):
        metas[k, :, 0:HD] = mk[:, HD * k : HD * k + HD]
        metas[k, :, HD : 2 * HD] = mv[:, HD * k : HD * k + HD]
        for j in range(GROUP):
            h = GROUP * k + j
            top = 2 * TOK * j
            qg[k, top : top + TOK, 0:HD] = (qs[:, HD * h : HD * h + HD].astype(F32) * 0.125).astype(BF)
            qg[k, top : top + TOK, HD : 2 * HD] = zeros
            qg[k, top + TOK : top + 2 * TOK, 0:HD] = zeros
            qg[k, top + TOK : top + 2 * TOK, HD : 2 * HD] = gs[:, HD * h : HD * h + HD]
    back = iota((TOK, TOK), 0) - iota((TOK, TOK), 1)
    never = jnp.int32(1 << 20)
    dist[:, 0:TOK] = jnp.zeros((TOK, TOK), jnp.int32)
    dist[:, TOK : 2 * TOK] = jnp.where(back >= 0, back, never)
    for d in range(1, 9):
        dist[:, TOK * (d + 1) : TOK * (d + 2)] = jnp.where(i >= d, back + TOK * d, never)
    pieces[0] = jnp.zeros((KVH, TOK, TOK), BF)
    pieces[9] = jnp.zeros((KVH, TOK, TOK), BF)

    def one(k, carry):
        kv = jnp.concatenate([metas[k], win[0:9, k].reshape(9 * TOK, TOK)], axis=0)
        for j in range(GROUP):
            h = GROUP * k + j
            top = 2 * TOK * j
            both = dot(qg[k, top : top + 2 * TOK, :], kv, NT)
            s, dp = both[:TOK], both[TOK:]
            s = jnp.where(dist[...] < wins[h], s, -1e30)
            e = jnp.exp(s - jnp.max(s, axis=1, keepdims=True))
            inv = 1.0 / jnp.sum(e, axis=1, keepdims=True)
            delta = jnp.sum(e * dp, axis=1, keepdims=True) * inv
            p = e * inv
            ds = (p * (dp - delta)).astype(BF)
            ps[top : top + TOK, :] = ds
            ps[top + TOK : top + 2 * TOK, :] = p.astype(BF)
            dqs[h] = dot(ds, kv)
        back_t = dot(qg[k], ps[...], TN)
        turned = back_t[:, :TOK].T
        sink[:, k] = turned.reshape(16, 8, TOK)
        own[k] = back_t[:, TOK : 2 * TOK]
        for d in range(1, 9):
            pieces[d, k] = back_t[:, TOK * (d + 1) : TOK * (d + 2)].astype(BF)
        return carry

    lax.fori_loop(0, KVH, one, 0)
    for h in range(HEADS):
        gq[:, HD * h : HD * h + HD] = (dqs[h, :, 0:HD] * 0.125).astype(BF)


def run_attention(windows, q, g, win, mk, mv):
    vm = pltpu.VMEM
    return pl.pallas_call(
        attention_kernel,
        out_shape=(
            jax.ShapeDtypeStruct((TOK, WIDTH), BF),
            jax.ShapeDtypeStruct((10, KVH, TOK, TOK), BF),
            jax.ShapeDtypeStruct((KVH, TOK, TOK), F32),
            jax.ShapeDtypeStruct((16, KVH, 8, TOK), F32),
        ),
        in_specs=[pl.BlockSpec(memory_space=pltpu.SMEM)] + [pl.BlockSpec(memory_space=vm)] * 5,
        out_specs=(pl.BlockSpec(memory_space=vm),) * 4,
        scratch_shapes=[
            vm((KVH, 2 * TOK * GROUP, TOK), BF),
            vm((KVH, TOK, TOK), BF),
            vm((TOK, 10 * TOK), jnp.int32),
            vm((2 * TOK * GROUP, 10 * TOK), BF),
            vm((HEADS, TOK, TOK), F32),
        ],
        compiler_params=pltpu.CompilerParams(vmem_limit_bytes=48 * 1024 * 1024),
        name="attention_grads",
    )(windows, q, g, win, mk, mv)


def grad_kernel(
    pieces, own, sink, gk, gv, gm,
    rc, ry, rz, sc, sb, sy, sa, k0, a0, k1, a1, k2, a2, k3, a3, k4, a4, k5,
    c_send, c_recv, kv_send, kv_recv, m_send, m_recv,
):
    dp, i, core, yh, z = places()
    c = i % 4
    zl, zh = z % 4, z // 4
    xx, yl = dp % 4, dp // 4
    up = ((z + 1) % 16) * 4 + c
    down = ((z + 15) % 16) * 4 + c
    base = i - c
    mate = base + (c + 1 - 2 * core)
    across = base + (c + 2) % 4
    near = [(dp, (zh * 4 + (zl + k) % 4) * 4 + c) for k in (1, 2, 3)]
    far = [(dp, (((zh + k) % 4) * 4 + zl) * 4 + c) for k in (1, 2, 3)]
    along_x = [(yl * 4 + (xx + k) % 4, i) for k in (1, 2, 3)]
    other = (1 - yl) * 4 + xx
    along_y = [(dp, across), (other, i), (other, across)]

    barrier = pltpu.get_barrier_semaphore()
    for to in [(dp, mate), (dp, up)] + near + far + along_x + along_y:
        pl.semaphore_signal(barrier, inc=1, device_id=to, device_id_type=MESH)
    pl.semaphore_wait(barrier, 14)

    def pair(src, dst, send, recv, n, to):
        return pltpu.make_async_remote_copy(
            src_ref=src, dst_ref=dst, send_sem=send.at[n], recv_sem=recv.at[n],
            device_id=to, device_id_type=MESH,
        )

    order = (8, 6, 2, 4, 0)
    mates = [
        pair(pieces.at[(d + core + 9 * (1 - core)) % 10], rc.at[n], c_send, c_recv, n, (dp, mate))
        for n, d in enumerate(order)
    ]
    for copy in mates[:2]:
        copy.start()
    m0 = pair(sink.at[1 - core], k0, m_send, m_recv, 0, (dp, mate))
    m0.start()
    for copy in mates[2:]:
        copy.start()

    step_c = pair(sc, rz.at[0], kv_send, kv_recv, 0, (dp, down))
    step_b = pair(sb, rz.at[1], kv_send, kv_recv, 1, (dp, down))
    step_y = pair(sy, ry, kv_send, kv_recv, 2, (dp, across))
    step_a = pair(sa, rz.at[2], kv_send, kv_recv, 3, (dp, down))

    mates[0].wait_recv()
    sc[...] = (pieces[8].astype(F32) + rc[0].astype(F32)).astype(BF)
    step_c.start()
    mates[1].wait_recv()
    sb[...] = (pieces[6].astype(F32) + rc[1].astype(F32)).astype(BF)
    step_b.start()

    m0.wait_recv()
    a0[...] = sink[core] + k0[...]
    m1 = [pair(a0.at[(xx + k) % 4], k1.at[n], m_send, m_recv, 1 + n, along_x[n]) for n, k in enumerate((1, 2, 3))]
    for copy in m1:
        copy.start()

    mates[2].wait_recv()
    sum_y = pieces[2].astype(F32) + rc[2].astype(F32)
    step_b.wait_recv()
    sy[...] = (sum_y + rz[1].astype(F32)).astype(BF)
    step_y.start()

    for copy in m1:
        copy.wait_recv()
    a1[...] = a0[xx] + k1[0] + k1[1] + k1[2]
    m2 = [
        pair(a1.at[yl if n == 0 else 1 - yl], k2.at[n], m_send, m_recv, 4 + n, along_y[n]) for n in range(3)
    ]
    for copy in m2:
        copy.start()

    mates[3].wait_recv()
    step_c.wait_recv()
    mates[4].wait_recv()

    for copy in m2:
        copy.wait_recv()
    a2[...] = a1[yl] + k2[0] + k2[1] + k2[2]
    m3 = [pair(a2, k3.at[n], m_send, m_recv, 7 + n, near[n]) for n in range(3)]
    for copy in m3:
        copy.start()

    step_y.wait_recv()
    here = jnp.where(yh == 1, 1.0, 0.0)
    sum_a = pieces[4].astype(F32) + rc[3].astype(F32) + rz[0].astype(F32)
    sa[...] = (sum_a + here * ry[...].astype(F32)).astype(BF)
    step_a.start()

    for copy in m3:
        copy.wait_recv()
    a3[...] = a2[...] + k3[0] + k3[1] + k3[2]
    m4 = [pair(a3, k4.at[n], m_send, m_recv, 10 + n, far[n]) for n in range(3)]
    for copy in m4:
        copy.start()
    mine = own[...] + rc[4].astype(F32) + (1.0 - here) * ry[...].astype(F32)
    for copy in m4:
        copy.wait_recv()
    a4[...] = a3[...] + k4[0] + k4[1] + k4[2]
    m5 = pair(a4, k5, m_send, m_recv, 13, (dp, mate))
    m5.start()

    step_a.wait_recv()
    mine = mine + rz[2].astype(F32)
    for k in range(KVH):
        turned = mine[k].T
        gk[:, HD * k : HD * k + HD] = turned[:, :HD].astype(BF)
        gv[:, HD * k : HD * k + HD] = turned[:, HD:].astype(BF)

    m5.wait_recv()
    lane, col = iota((TOK, TOK), 0), iota((TOK, TOK), 1)
    first = jnp.zeros((8, TOK), F32)
    second = jnp.zeros((8, TOK), F32)
    for k in range(KVH):
        feature = 5 * i + col % 8 - HD * k
        pick = (col % 8 < 5) & (col < 16) & (feature >= 0) & (feature < HD) & (lane == feature + HD * (col // 8))
        pick = pick.astype(BF)
        mine_k, other_k = a4[k], k5[k]
        first = first + dot3(mine_k, pick)
        second = second + dot3(other_k, pick)
    top = jnp.where(core == 0, first, second)
    low = jnp.where(core == 0, second, first)
    gm[0, 0:8] = top[:, 0:5]
    gm[0, 8:16] = low[:, 0:5]
    gm[1, 0:8] = top[:, 8:13]
    gm[1, 8:16] = low[:, 8:13]

    for copy in mates + [m0, step_a, step_b, step_c, step_y] + m1 + m2 + m3 + m4 + [m5]:
        copy.wait_send()


def run_grads(pieces, own, sink):
    dma = pltpu.SemaphoreType.DMA
    vm = pltpu.VMEM
    block = (KVH, TOK, TOK)
    part = (KVH, 8, TOK)
    return pl.pallas_call(
        grad_kernel,
        out_shape=(
            jax.ShapeDtypeStruct((TOK, KVW), BF),
            jax.ShapeDtypeStruct((TOK, KVW), BF),
            jax.ShapeDtypeStruct((2, 16, 5), F32),
        ),
        in_specs=[pl.BlockSpec(memory_space=vm)] * 3,
        out_specs=(pl.BlockSpec(memory_space=vm),) * 3,
        scratch_shapes=[
            vm((5,) + block, BF), vm(block, BF), vm((3,) + block, BF),
            vm(block, BF), vm(block, BF), vm(block, BF), vm(block, BF),
            vm((4, 2) + part, F32), vm((4, 2) + part, F32),
            vm((3, 2) + part, F32), vm((2,) + part, F32),
            vm((3,) + part, F32), vm(part, F32),
            vm((3,) + part, F32), vm(part, F32),
            vm((3,) + part, F32), vm(part, F32),
            vm(part, F32),
            dma((5,)), dma((5,)), dma((4,)), dma((4,)), dma((14,)), dma((14,)),
        ],
        compiler_params=pltpu.CompilerParams(
            collective_id=1, has_side_effects=True, vmem_limit_bytes=40 * 1024 * 1024
        ),
        name="gradient_sums",
    )(pieces, own, sink)


def local(
    queries, key_vectors, value_vectors, meta_keys, meta_values, windows,
    ssm_input, input_map, output_map, log_decay, cotangent,
):
    win, grad_input, grad_bm, grad_cm = run_ctx(
        key_vectors[0], value_vectors[0], ssm_input[0], cotangent[0], input_map[0], output_map[0], log_decay[0]
    )
    grad_q, pieces, own, sink = run_attention(windows, queries[0], cotangent[0], win, meta_keys, meta_values)
    sink = sink.reshape(2, 4, 2, KVH, 8, TOK).transpose(2, 1, 0, 3, 4, 5)
    grad_k, grad_v, grad_meta = run_grads(pieces, own, sink)
    return (
        grad_q[None], grad_k[None], grad_v[None], grad_meta, grad_input[None], grad_bm[None], grad_cm[None],
    )


def solution(mesh):
    seq = P("dp", "ctx", None)
    return jax.shard_map(
        local,
        mesh=mesh,
        in_specs=(seq, seq, seq, P(), P(), P(), seq, seq, seq, seq, seq),
        out_specs=(seq, seq, seq, P(None, "dp", "ctx"), seq, seq, seq),
        check_vma=False,
    )
```

time: 690 us -> 131 us (0.19); the launches traced: 680 us -> 130 us
  blocking collectives: 344 us -> 0 us
  other arithmetic: 150 us -> 0 us
  Pallas kernels: 0 us -> 101 us
  matrix products: 73.1 us -> 0 us
  starting transfers between devices: 51.8 us -> 0 us
  waiting for transfers between devices: 23.5 us -> 0 us
  between operations: 17.3 us -> 0.76 us
  local copies, waits for them, and re-layouts: 14.7 us -> 28.1 us
    unnamed x1 -> x0, blocking collectives: 255 us -> none
    select_n x128 -> x0, other arithmetic: 134 us -> none  [turn(): return jax.tree.map(lambda a, b: jnp.where(reached, a, b), new, before)]
    pallas_call x0 -> x3, Pallas kernels: none -> 101 us  [the longest x1 43.6 us: run_ctx(): pl.pallas_call(ctx_kernel, out_shape=(jax.ShapeDtypeStruct((10, KVH, TOK,...]
    all_gather x1 -> x0, blocking collectives: 88.3 us -> none  [entering(): everything = jax.tree.map(lambda part: lax.all_gather(part, axis), shard)]
    dot_general x70 -> x0, matrix products: 73.1 us -> none  [the longest x5 11.3 us: head_terms(): jnp.einsum('gqe,ke->gqk', grad_h, value_h, preferred_element_type=jnp.flo...]
    ppermute x16 -> x0, starting transfers between devices: 51.7 us -> none  [from_behind(): return lax.ppermute(shard, axis, pairs)]
    ppermute x16 -> x0, waiting for transfers between devices: 23.5 us -> none  [from_behind(): return lax.ppermute(shard, axis, pairs)]
    unnamed x36 -> x43, local copies, waits for them, and re-layouts: 6.25 us -> 27.1 us
  transfers between devices with their start and end apart: 19 -> 0, of which waited for: 4 -> 0; matrix products, arithmetic and copies ran while one was open for 12% -> 0% of each run, Pallas kernels for 0% -> 0%
where the time goes in v1:
time: 131 us; the launch traced here: 130 us
  Pallas kernels  101 us (77%)
  local copies, waits for them, and re-layouts  28.1 us (21%)
    pallas_call x1, Pallas kernels, run_ctx(): pl.pallas_call(ctx_kernel, out_shape=(jax.ShapeDtypeStruct((10, KVH, TOK,...  43.6 us
    pallas_call x1, Pallas kernels, run_grads(): pl.pallas_call(grad_kernel, out_shape=(jax.ShapeDtypeStruct((TOK, KVW), B...  36.5 us
    unnamed x43, local copies, waits for them, and re-layouts  27.1 us
    pallas_call x1, Pallas kernels, run_attention(): pl.pallas_call(attention_kernel, out_shape=(jax.ShapeDtypeStruct((TOK, WI...  21.4 us

profile of v1, /device:TPU:1, one launch (start us, length us, event | category | flops | bytes accessed | tf_op | source)
XLA Modules:
  0.0 130.3 jit_solution(7245800185826161800)
XLA Ops:
  0.7 1.5 %copy.40 = bf16[1,128,16]{2,1,0:T(8,128)(2,1)} copy(bf16[1,128,16]{1,2,0:T(8,128)(2,1)} %param.18) | data formatting | bytes 8192 | tf_op args[7]
  2.1 1.4 %copy.41 = bf16[1,128,16]{2,1,0:T(8,128)(2,1)} copy(bf16[1,128,16]{1,2,0:T(8,128)(2,1)} %param.19) | data formatting | bytes 8192 | tf_op args[8]
  3.5 1.4 %copy.42 = f32[1,128,25]{2,1,0:T(8,128)} copy(f32[1,128,25]{1,0,2:T(1,128)} %param.20) | data formatting | bytes 25600 | tf_op args[9]
  5.0 1.6 %copy.37 = bf16[1,128,320]{2,1,0:T(8,128)(2,1)} copy(bf16[1,128,320]{1,2,0:T(8,128)(2,1)} %param.12) | data formatting | bytes 163840 | tf_op args[1]
  6.6 1.6 %copy.38 = bf16[1,128,320]{2,1,0:T(8,128)(2,1)} copy(bf16[1,128,320]{1,2,0:T(8,128)(2,1)} %param.13) | data formatting | bytes 163840 | tf_op args[2]
  8.2 1.0 copy.43.mk
  9.2 1.0 copy.44.mv
  10.2 1.2 copy.35
  12.0 0.9 copy-done.2
  12.9 0.9 copy-done.3
  13.8 0.8 copy-done.5
  14.7 0.8 copy-done.6
  15.4 0.8 copy-done.7
  16.2 43.6 %halo_and_scan.1 = (bf16[10,5,128,128]{3,2,1,0:T(8,128)(2,1)S(1)}, bf16[128,1600]{1,0:T(8,128)(2,1)S(1)}, f32[128,16]{1,0:T(8,128)S(1)}, f32[128,16]{1,0:T(8,128)S(1)}) custom-call(bf16[128,320]{1,0:T(8,128)(2,1)S(1)} %bitcast.25, bf16[128,320]{1,0:T(8,128)(2,1)S(1)} %bitcast.26, bf16[128,1600]{1,0:T(8,128)(2,1)S(1)} %bitcast.21, ...), custom_call_target="tpu_custom_call" | custom-call | tf_op jit(solution)/shard_map/halo_and_scan/pallas_call | solution.py:275
  61.0 0.9 copy.50
  61.9 1.5 %copy.51 = f32[1,128,16]{1,2,0:T(8,128)} copy(f32[1,128,16]{2,1,0:T(8,128)} %bitcast.34) | data formatting | bytes 16384
  63.5 1.5 %copy.52 = f32[1,128,16]{1,2,0:T(8,128)} copy(f32[1,128,16]{2,1,0:T(8,128)} %bitcast.33) | data formatting | bytes 16384
  65.0 21.4 %attention_grads.1 = (bf16[128,1600]{1,0:T(8,128)(2,1)S(1)}, bf16[10,5,128,128]{3,2,1,0:T(8,128)(2,1)S(1)}, f32[5,128,128]{2,1,0:T(8,128)S(1)}, f32[16,5,8,128]{3,2,1,0:T(8,128)S(1)}) custom-call(s32[25]{0:T(128)S(1)} %copy-done.10, bf16[128,1600]{1,0:T(8,128)(2,1)S(1)} %bitcast.20, bf16[128,1600]{1,0:T(8,128)(2,1)S(1)} %bitcast.19, ...), custom_call_target="tpu_custom_call" | custom-call | tf_op jit(solution)/shard_map/attention_grads/pallas_call | solution.py:371
  86.4 1.2 copy-done
  88.3 0.9 copy.46
  89.3 1.0 copy.54
  90.3 1.4 %copy-done.1 = bf16[10,5,128,128]{3,2,1,0:T(8,128)(2,1)S(1)} copy-done((bf16[10,5,128,128]{3,2,1,0:T(8,128)(2,1)S(1)}, bf16[10,5,128,128]{3,2,1,0:T(8,128)(2,1)}, u32[]{:S(2)}) %copy-start.1) | copy-done | bytes 1638424
  91.7 36.5 %gradient_sums.1 = (bf16[128,320]{1,0:T(8,128)(2,1)S(1)}, bf16[128,320]{1,0:T(8,128)(2,1)S(1)}, f32[2,16,5]{2,1,0:T(8,128)S(1)}) custom-call(bf16[10,5,128,128]{3,2,1,0:T(8,128)(2,1)S(1)} %copy-done.1, f32[5,128,128]{2,1,0:T(8,128)S(1)} %get-tuple-element.21.own, f32[2,4,2,5,8,128]{5,4,3,2,1,0:T(8,128)S(1)} %bitcast.22), custom_call_target="tpu_custom_call" | custom-call | tf_op jit(solution)/shard_map/gradient_sums/pallas_call | solution.py:533
  128.1 0.7 copy.47
  (23 shorter events, 3.9 us)
Async XLA Ops:
  0.6 11.1 %copy-start.12 = (bf16[1,128,1600]{1,2,0:T(8,128)(2,1)S(1)}, bf16[1,128,1600]{1,2,0:T(8,128)(2,1)}, u32[]{:S(2)}) copy-start(bf16[1,128,1600]{1,2,0:T(8,128)(2,1)} %param.21) | copy-start | bytes 1228804
  0.6 10.8 %copy-start.11 = (bf16[1,128,1600]{1,2,0:T(8,128)(2,1)S(1)}, bf16[1,128,1600]{1,2,0:T(8,128)(2,1)}, u32[]{:S(2)}) copy-start(bf16[1,128,1600]{1,2,0:T(8,128)(2,1)} %param.17) | copy-start | bytes 1228804
  11.7 53.2 %copy-start.10 = (s32[25]{0:T(128)S(1)}, s32[25]{0:T(128)}, u32[]{:S(2)}) copy-start(s32[25]{0:T(128)} %wins.1) | copy-start | bytes 304
  12.0 0.9 copy-start.2
  12.9 0.9 copy-start.3
  13.8 0.8 copy-start.5
  14.6 0.8 copy-start.6
  15.4 0.8 copy-start.7
  59.7 0.6 copy-start.8
  60.4 0.6 copy-start.9
  86.4 1.2 copy-start
  87.6 0.7 copy-start.4
  90.3 1.4 %copy-start.1 = (bf16[10,5,128,128]{3,2,1,0:T(8,128)(2,1)S(1)}, bf16[10,5,128,128]{3,2,1,0:T(8,128)(2,1)}, u32[]{:S(2)}) copy-start(bf16[10,5,128,128]{3,2,1,0:T(8,128)(2,1)} %copy-done) | copy-start | bytes 4915204

commit v2 on v0

v2 whole, which is shorter than its diff:
```python
import functools

import jax
import jax.numpy as jnp
from jax import lax
from jax.experimental import pallas as pl
from jax.experimental.pallas import tpu as pltpu
from jax.sharding import PartitionSpec as P

BF = jnp.bfloat16
F32 = jnp.float32
MESH = pl.DeviceIdType.MESH
HEADS, KVH, GROUP, HD = 25, 5, 5, 64
TOK, WIDTH, KVW, STATE = 128, 1600, 320, 16
QL = 448
NT = (((1,), (1,)), ((), ()))
TN = (((0,), (0,)), ((), ()))


def dot(a, b, dims=(((1,), (0,)), ((), ()))):
    return lax.dot_general(a, b, dims, preferred_element_type=F32)


def split3(v):
    hi = v.astype(BF)
    rest = v - hi.astype(F32)
    mid = rest.astype(BF)
    low = (rest - mid.astype(F32)).astype(BF)
    return hi, mid, low


def dot3(v, onehot):
    hi, mid, low = split3(v)
    return dot(hi, onehot) + dot(mid, onehot) + dot(low, onehot)


def iota(shape, dim):
    return lax.broadcasted_iota(jnp.int32, shape, dim)


def places():
    dp, i = lax.axis_index("dp"), lax.axis_index("ctx")
    return dp, i, i % 2, (i // 2) % 2, i // 4


def layer_kernel(
    wins, key, val, xin, gin_, qin, bmin, cmin, ldin, mkin, mvin,
    gq, gk, gv, gm, gin, gbm, gcm,
    x, g, q, bm, cm, ldv, ldp, xt, gt, loc, win, metas, qg, dist, ps, pieces, own, sink,
    stq, r1, d0, d1, s2, r2, d2s, d2, s3, r3, d3s, d3, ib, ob, inc, adj,
    rc, ry, rz, sc, sb, sy, sa, k0, a0, k1, a1, k2, a2, k3, a3, k4, a4, k5,
    in_sem, kv_send, kv_recv, c_send, c_recv, q1_send, q1_recv, q2_send, q2_recv, q3_send, q3_recv,
    q4_send, q4_recv, e_send, e_recv, t_send, t_recv, m_send, m_recv,
):
    dp, i, core, yh, z = places()
    c = i % 4
    zl, zh = z % 4, z // 4
    xx, yl = dp % 4, dp // 4
    base = i - c
    ahead2, ahead4 = (i + 2) % 64, (i + 4) % 64
    back2, back4 = (i + 62) % 64, (i + 60) % 64
    group = [base + (c + k) % 4 for k in (1, 2, 3)]
    near = [(zh * 4 + (zl + k) % 4) * 4 + c for k in (1, 2, 3)]
    far = [(((zh + k) % 4) * 4 + zl) * 4 + c for k in (1, 2, 3)]
    mate = base + (c + 1 - 2 * core)
    across = base + (c + 2) % 4
    along_x = [(yl * 4 + (xx + k) % 4, i) for k in (1, 2, 3)]
    other = (1 - yl) * 4 + xx
    along_y = [(dp, across), (other, i), (other, across)]

    barrier = pltpu.get_barrier_semaphore()
    here = [(dp, to) for to in group + near + far + [ahead2, ahead4, back2, back4]]
    for to in here + along_x + along_y[1:]:
        pl.semaphore_signal(barrier, inc=1, device_id=to, device_id_type=MESH)

    def fetch(n, src, dst):
        copy = pltpu.make_async_copy(src, dst, in_sem.at[n])
        copy.start()
        return copy

    first_in = [fetch(0, key, win.at[0, :, 0:HD, :]), fetch(1, val, win.at[0, :, HD : 2 * HD, :])]
    scan_in = [fetch(2, ldin, ldv), fetch(3, xin, x), fetch(4, gin_, g), fetch(5, bmin, bm), fetch(6, cmin, cm)]
    late_in = [
        fetch(7, qin, q), fetch(8, mkin, metas.at[:, 0:HD, :]), fetch(9, mvin, metas.at[:, HD : 2 * HD, :])
    ]

    def pair(src, dst, send, recv, n, to):
        return pltpu.make_async_remote_copy(
            src_ref=src, dst_ref=dst, send_sem=send.at[n], recv_sem=recv.at[n],
            device_id=to, device_id_type=MESH,
        )

    for copy in scan_in:
        copy.wait()
    rows, cols = iota((TOK, TOK), 0), iota((TOK, TOK), 1)
    tri = (rows >= cols).astype(BF)
    ldp[...] = jnp.zeros((32, TOK), F32)
    for h in range(HEADS):
        ldp[h : h + 1, :] = ldv[h]
    run = jnp.zeros((TOK, 32), F32)
    run_t = jnp.zeros((32, TOK), F32)
    for part in split3(ldp[...]):
        run = run + dot(tri, part, NT)
        run_t = run_t + dot(part, tri, NT)
    end = run_t[:, TOK - 1 : TOK]
    tail = jnp.exp(end - run_t)
    head = jnp.exp(run_t)
    for h in range(HEADS):
        f = slice(HD * h, HD * h + HD)
        xt[f, :] = (tail[h : h + 1, :] * x[f, :].astype(F32)).astype(BF)
        gt[f, :] = (head[h : h + 1, :] * g[f, :].astype(F32)).astype(BF)
    for w, terms in enumerate((dot(bm[...], xt[...], NT), dot(cm[...], gt[...], NT))):
        for p in range(4):
            n = min(QL, WIDTH - QL * p)
            stq[p, w] = jnp.concatenate(
                [terms[:, QL * p : QL * p + n], jnp.zeros((STATE, 512 - n), F32)], axis=1
            ).astype(BF)
    d0[...] = jnp.broadcast_to(jnp.exp(run[TOK - 1 : TOK, :]), (8, 32))
    for copy in first_in:
        copy.wait()
    pl.semaphore_wait(barrier, 18)

    def mate_copy(d, n):
        return pair(win.at[d], win.at[(d + core * 9 + (1 - core)) % 10], c_send, c_recv, n, (dp, mate))

    step_a = pair(win.at[0], win.at[4], kv_send, kv_recv, 0, (dp, ahead4))
    step_y = pair(win.at[0], win.at[2], kv_send, kv_recv, 1, (dp, ahead2))
    step_b = pair(win.at[2], win.at[6], kv_send, kv_recv, 2, (dp, ahead4))
    step_c = pair(win.at[4], win.at[8], kv_send, kv_recv, 3, (dp, ahead4))
    mates = [mate_copy(d, n) for n, d in enumerate((0, 4, 2, 8, 6))]
    step_y.start()
    step_a.start()
    mates[0].start()

    q1 = []
    for n, k in enumerate((1, 2, 3)):
        q1.append(pair(stq.at[(c + k) % 4], r1.at[c], q1_send, q1_recv, n, (dp, group[n])))
        q1.append(pair(d0, d1.at[c], q1_send, q1_recv, 3 + n, (dp, group[n])))
    for copy in q1:
        copy.start()
    r1[c] = stq[c]
    d1[c] = d0[...]

    inner = dot(cm[...], bm[...], TN)

    def local_head(h, gram):
        f = slice(HD * h, HD * h + HD)
        diff = run[:, h : h + 1] - run_t[h : h + 1, :]
        mix = jnp.where(rows >= cols, jnp.exp(diff), 0.0)
        loc[f, :] = dot(g[f, :], (mix * inner).astype(BF))
        return gram + mix * dot(g[f, :], x[f, :], TN)

    gram = jnp.zeros((TOK, TOK), F32)
    for h in range(0, 10):
        gram = local_head(h, gram)
    step_a.wait_recv()
    step_c.start()
    mates[1].start()
    for h in range(10, 18):
        gram = local_head(h, gram)
    step_y.wait_recv()
    step_b.start()
    mates[2].start()

    row, lane = iota((32, 512), 0), iota((32, 512), 1)
    onehot = ((row == 7 * c + lane // HD) & (lane < QL)).astype(BF)

    def expand(d):
        wide = dot3(d[...].reshape(32, 32), onehot)
        return [jnp.broadcast_to(wide[8 * j : 8 * j + 1], (STATE, 512)) for j in range(4)]

    def sums(dec, terms):
        total, back = terms[0, 0].astype(F32), terms[3, 1].astype(F32)
        for j in range(1, 4):
            total = dec[j] * total + terms[j, 0].astype(F32)
            back = dec[3 - j] * back + terms[3 - j, 1].astype(F32)
        return total.astype(BF), back.astype(BF)

    q2 = []
    for n in range(3):
        q2.append(pair(s2, r2.at[zl], q2_send, q2_recv, n, (dp, near[n])))
        q2.append(pair(d2s, d2.at[zl], q2_send, q2_recv, 3 + n, (dp, near[n])))
    q3 = []
    for n, k in enumerate((1, 2, 3)):
        there = (zh + k) % 4
        which = jnp.where(there > zh, 0, 1)
        q3.append(pair(s3.at[which], r3.at[zh], q3_send, q3_recv, n, (dp, far[n])))
        q3.append(pair(d3s, d3.at[zh], q3_send, q3_recv, 3 + n, (dp, far[n])))
    q4 = [
        pair(ib.at[(c + k) % 4], ob.at[c], q4_send, q4_recv, n, (dp, group[n]))
        for n, k in enumerate((1, 2, 3))
    ]

    def scan_second():
        for copy in q1:
            copy.wait_recv()
        s2[0], s2[1] = sums(expand(d1), r1)
        d2s[...] = d1[0] * d1[1] * d1[2] * d1[3]
        for copy in q2:
            copy.start()
        r2[zl] = s2[...]
        d2[zl] = d2s[...]

    def scan_third():
        for copy in q2:
            copy.wait_recv()
        s3[0], s3[1] = sums(expand(d2), r2)
        d3s[...] = d2[0] * d2[1] * d2[2] * d2[3]
        for copy in q3:
            copy.start()
        r3[zh] = s3[0]
        d3[zh] = d3s[...]

    def scan_fourth():
        for copy in q3:
            copy.wait_recv()
        dec1, dec2, dec3 = expand(d1), expand(d2), expand(d3)
        ahead = jnp.zeros((STATE, 512), F32)
        behind = ahead
        for j in range(4):
            b = 3 - j
            ahead = jnp.where(j < zh, dec3[j] * ahead + r3[j].astype(F32), ahead)
            behind = jnp.where(b > zh, dec3[b] * behind + r3[b].astype(F32), behind)
        for j in range(4):
            b = 3 - j
            ahead = jnp.where(j < zl, dec2[j] * ahead + r2[j, 0].astype(F32), ahead)
            behind = jnp.where(b > zl, dec2[b] * behind + r2[b, 1].astype(F32), behind)
        for j in range(4):
            b = 3 - j
            ib[j, 0] = ahead.astype(BF)
            ahead = dec1[j] * ahead + r1[j, 0].astype(F32)
            ib[b, 1] = behind.astype(BF)
            behind = dec1[b] * behind + r1[b, 1].astype(F32)
        for copy in q4:
            copy.start()
        ob[c] = ib[c]

    scan_second()
    for h in range(18, HEADS):
        gram = local_head(h, gram)
    gram = gram.astype(BF)
    gbm[...] = dot(cm[...], gram)
    gcm[...] = dot(bm[...], gram, NT)

    for copy in late_in:
        copy.wait()
    zeros = jnp.zeros((HD, TOK), BF)
    for k in range(KVH):
        for j in range(GROUP):
            f = slice(HD * (GROUP * k + j), HD * (GROUP * k + j) + HD)
            at = 2 * TOK * j
            qg[k, 0:HD, at : at + TOK] = (q[f, :].astype(F32) * 0.125).astype(BF)
            qg[k, 0:HD, at + TOK : at + 2 * TOK] = zeros
            qg[k, HD : 2 * HD, at : at + TOK] = zeros
            qg[k, HD : 2 * HD, at + TOK : at + 2 * TOK] = g[f, :]
    behind_by = rows - cols
    never = jnp.int32(1 << 20)
    dist[:, 0:TOK] = jnp.zeros((TOK, TOK), jnp.int32)
    dist[:, TOK : 2 * TOK] = jnp.where(behind_by >= 0, behind_by, never)
    for d in range(1, 9):
        dist[:, TOK * (d + 1) : TOK * (d + 2)] = jnp.where(i >= d, behind_by + TOK * d, never)
    pieces[9] = jnp.zeros((KVH, TOK, TOK), BF)

    step_c.wait_recv()
    mates[3].start()
    step_b.wait_recv()
    mates[4].start()
    for copy in mates:
        copy.wait_recv()

    def keys_of(k):
        return jnp.concatenate([metas[k]] + [win[d, k] for d in range(9)], axis=1)

    def probs_of(k, carry):
        kv = keys_of(k)
        for j in range(GROUP):
            at = 2 * TOK * j
            both = dot(qg[k, :, at : at + 2 * TOK], kv, TN)
            s, dpr = both[:TOK], both[TOK:]
            s = jnp.where(dist[...] < wins[GROUP * k + j], s, -1e30)
            e = jnp.exp(s - jnp.max(s, axis=1, keepdims=True))
            inv = 1.0 / jnp.sum(e, axis=1, keepdims=True)
            delta = jnp.sum(e * dpr, axis=1, keepdims=True) * inv
            p = e * inv
            ps[k, at : at + TOK, :] = (p * (dpr - delta)).astype(BF)
            ps[k, at + TOK : at + 2 * TOK, :] = p.astype(BF)
        turned = dot(qg[k], ps[k, :, 0:TOK]).T
        for r in range(16):
            sink[r % 2, (r // 2) % 4, r // 8, k] = turned[8 * r : 8 * r + 8]

        @pl.when(k == 0)
        def _():
            scan_third()

        @pl.when(k == 3)
        def _():
            scan_fourth()

        return carry

    lax.fori_loop(0, KVH, probs_of, 0)

    m0 = pair(sink.at[1 - core], k0, m_send, m_recv, 0, (dp, mate))
    m1 = [pair(a0.at[(xx + k) % 4], k1.at[n], m_send, m_recv, 1 + n, along_x[n]) for n, k in enumerate((1, 2, 3))]
    m2 = [pair(a1.at[yl if n == 0 else 1 - yl], k2.at[n], m_send, m_recv, 4 + n, along_y[n]) for n in range(3)]
    m3 = [pair(a2, k3.at[n], m_send, m_recv, 7 + n, (dp, near[n])) for n in range(3)]
    m4 = [pair(a3, k4.at[n], m_send, m_recv, 10 + n, (dp, far[n])) for n in range(3)]
    m5 = pair(a4, k5, m_send, m_recv, 13, (dp, mate))

    def pass_on(arrived, result, value, following):
        for copy in arrived:
            copy.wait_recv()
        result[...] = value()
        for copy in following:
            copy.start()

    m0.start()

    def grads_of(k, carry):
        kv = keys_of(k)
        for j in range(GROUP):
            at = 2 * TOK * j
            dq = dot(kv[0:HD], ps[k, at : at + TOK, :], NT) * 0.125
            gq[pl.ds(pl.multiple_of(HD * (GROUP * k + j), HD), HD), :] = dq.astype(BF)
        back_t = dot(qg[k], ps[k, :, TOK:])
        own[k] = back_t[:, :TOK]
        for d in range(1, 9):
            pieces[d, k] = back_t[:, TOK * d : TOK * (d + 1)].astype(BF)

        @pl.when(k == 0)
        def _():
            pass_on([m0], a0, lambda: sink[core] + k0[...], m1)

        @pl.when(k == 2)
        def _():
            pass_on(m1, a1, lambda: a0[xx] + k1[0] + k1[1] + k1[2], m2)

        @pl.when(k == 4)
        def _():
            pass_on(m2, a2, lambda: a1[yl] + k2[0] + k2[1] + k2[2], m3)

        return carry

    lax.fori_loop(0, KVH, grads_of, 0)

    give = [
        pair(pieces.at[(d + core + 9 * (1 - core)) % 10], rc.at[n], e_send, e_recv, n, (dp, mate))
        for n, d in enumerate((8, 6, 2, 4, 0))
    ]
    for copy in give:
        copy.start()
    back_c = pair(sc, rz.at[0], t_send, t_recv, 0, (dp, back4))
    back_b = pair(sb, rz.at[1], t_send, t_recv, 1, (dp, back4))
    back_y = pair(sy, ry, t_send, t_recv, 2, (dp, back2))
    back_a = pair(sa, rz.at[2], t_send, t_recv, 3, (dp, back4))
    give[1].wait_recv()
    sb[...] = (pieces[6].astype(F32) + rc[1].astype(F32)).astype(BF)
    back_b.start()
    give[0].wait_recv()
    sc[...] = (pieces[8].astype(F32) + rc[0].astype(F32)).astype(BF)
    back_c.start()
    pass_on(m3, a3, lambda: a2[...] + k3[0] + k3[1] + k3[2], m4)

    for copy in q4:
        copy.wait_recv()
    for p in range(4):
        n = min(QL, WIDTH - QL * p)
        inc[:, QL * p : QL * p + n] = ob[p, 0].astype(F32)[:, :n]
        adj[:, QL * p : QL * p + n] = ob[p, 1].astype(F32)[:, :n]
    inc_h, adj_h = inc[...].astype(BF), adj[...].astype(BF)
    gbm[...] = gbm[...] + dot(adj_h, xt[...])
    gcm[...] = gcm[...] + dot(inc_h, gt[...])

    for copy in give[2:]:
        copy.wait_recv()
    sum_y = pieces[2].astype(F32) + rc[2].astype(F32)
    back_b.wait_recv()
    sy[...] = (sum_y + rz[1].astype(F32)).astype(BF)
    back_y.start()
    sum_a = pieces[4].astype(F32) + rc[3].astype(F32)
    back_c.wait_recv()
    sa[...] = (sum_a + rz[0].astype(F32)).astype(BF)
    back_a.start()

    carried = dot(adj_h, bm[...], TN)
    tail = jnp.exp(end - run_t)
    for h in range(HEADS):
        f = slice(HD * h, HD * h + HD)
        gin[f, :] = (loc[f, :] + tail[h : h + 1, :] * carried[f]).astype(BF)

    pass_on(m4, a4, lambda: a3[...] + k4[0] + k4[1] + k4[2], [m5])
    back_y.wait_recv()
    back_a.wait_recv()
    for k in range(KVH):
        mine = own[k] + rc[4, k].astype(F32) + ry[k].astype(F32) + rz[2, k].astype(F32)
        gk[HD * k : HD * k + HD, :] = mine[:HD].astype(BF)
        gv[HD * k : HD * k + HD, :] = mine[HD:].astype(BF)

    m5.wait_recv()
    row, lane = iota((16, TOK), 0), iota((16, TOK), 1)
    first = jnp.zeros((16, 8), F32)
    second = jnp.zeros((16, 8), F32)
    for k in range(KVH):
        feature = 5 * i + row % 8 - HD * k
        pick = (row % 8 < 5) & (feature >= 0) & (feature < HD) & (lane == feature + HD * (row // 8))
        pick = pick.astype(BF)
        for part in split3(a4[k]):
            first = first + dot(pick, part, NT)
        for part in split3(k5[k]):
            second = second + dot(pick, part, NT)
    left = jnp.where(core == 0, first, second)
    right = jnp.where(core == 0, second, first)
    for j in range(5):
        for w in range(2):
            gm[j, w : w + 1, 0:8] = left[8 * w + j : 8 * w + j + 1]
            gm[j, w : w + 1, 8:16] = right[8 * w + j : 8 * w + j + 1]

    for copy in [step_a, step_y, step_b, step_c] + mates + q1 + q2 + q3 + q4:
        copy.wait_send()
    for copy in give + [back_a, back_b, back_c, back_y, m0, m5] + m1 + m2 + m3 + m4:
        copy.wait_send()


OUTS = (
    ((WIDTH, TOK), BF), ((KVW, TOK), BF), ((KVW, TOK), BF), ((5, 2, 16), F32),
    ((WIDTH, TOK), BF), ((STATE, TOK), F32), ((STATE, TOK), F32),
)


def run_layer(*args):
    dma = pltpu.SemaphoreType.DMA
    vm = pltpu.VMEM
    block = (KVH, TOK, TOK)
    part = (KVH, 8, TOK)
    quarter = (2, STATE, 512)
    return pl.pallas_call(
        layer_kernel,
        out_shape=tuple(jax.ShapeDtypeStruct(s, t) for s, t in OUTS),
        in_specs=[pl.BlockSpec(memory_space=pltpu.SMEM)] + [pl.BlockSpec(memory_space=pl.ANY)] * 10,
        out_specs=(pl.BlockSpec(memory_space=vm),) * 7,
        scratch_shapes=[
            vm((WIDTH, TOK), BF), vm((WIDTH, TOK), BF), vm((WIDTH, TOK), BF),
            vm((STATE, TOK), BF), vm((STATE, TOK), BF), vm((HEADS, 1, TOK), F32), vm((32, TOK), F32),
            vm((WIDTH, TOK), BF), vm((WIDTH, TOK), BF), vm((WIDTH, TOK), F32),
            vm((10,) + block, BF), vm(block, BF), vm((KVH, TOK, 2 * TOK * GROUP), BF),
            vm((TOK, 10 * TOK), jnp.int32), vm((KVH, 2 * TOK * GROUP, 10 * TOK), BF),
            vm((10,) + block, BF), vm(block, F32), vm((2, 4, 2) + part, F32),
            vm((4,) + quarter, BF), vm((4,) + quarter, BF), vm((8, 32), F32), vm((4, 8, 32), F32),
            vm(quarter, BF), vm((4,) + quarter, BF), vm((8, 32), F32), vm((4, 8, 32), F32),
            vm(quarter, BF), vm((4, STATE, 512), BF), vm((8, 32), F32), vm((4, 8, 32), F32),
            vm((4,) + quarter, BF), vm((4,) + quarter, BF), vm((STATE, WIDTH), F32), vm((STATE, WIDTH), F32),
            vm((5,) + block, BF), vm(block, BF), vm((3,) + block, BF),
            vm(block, BF), vm(block, BF), vm(block, BF), vm(block, BF),
            vm((4, 2) + part, F32), vm((4, 2) + part, F32),
            vm((3, 2) + part, F32), vm((2,) + part, F32),
            vm((3,) + part, F32), vm(part, F32),
            vm((3,) + part, F32), vm(part, F32),
            vm((3,) + part, F32), vm(part, F32),
            vm(part, F32),
            dma((10,)), dma((4,)), dma((4,)), dma((5,)), dma((5,)),
            dma((6,)), dma((6,)), dma((6,)), dma((6,)), dma((6,)), dma((6,)), dma((3,)), dma((3,)),
            dma((5,)), dma((5,)), dma((4,)), dma((4,)), dma((14,)), dma((14,)),
        ],
        compiler_params=pltpu.CompilerParams(
            collective_id=0, has_side_effects=True, vmem_limit_bytes=56 * 1024 * 1024
        ),
        name="layer_grads",
    )(*args)


def hand_out_kernel(*refs):
    sources, targets, through, sem = refs[:7], refs[7:14], refs[14:21], refs[21]
    arrive = [pltpu.make_async_copy(a, b, sem.at[n]) for n, (a, b) in enumerate(zip(sources, through))]
    leave = [pltpu.make_async_copy(a, b, sem.at[7 + n]) for n, (a, b) in enumerate(zip(through, targets))]
    for copy in arrive:
        copy.start()
    for first, then in zip(arrive, leave):
        first.wait()
        then.start()
    for copy in leave:
        copy.wait()


def hand_out(arrays):
    return pl.pallas_call(
        hand_out_kernel,
        out_shape=tuple(jax.ShapeDtypeStruct(s, t) for s, t in OUTS),
        in_specs=[pl.BlockSpec(memory_space=pl.ANY)] * 7,
        out_specs=(pl.BlockSpec(memory_space=pl.ANY),) * 7,
        scratch_shapes=[pltpu.VMEM(s, t) for s, t in OUTS] + [pltpu.SemaphoreType.DMA((14,))],
        compiler_params=pltpu.CompilerParams(vmem_limit_bytes=60 * 1024 * 1024),
        name="hand_out",
    )(*arrays)


def local(
    queries, key_vectors, value_vectors, meta_keys, meta_values, windows,
    ssm_input, input_map, output_map, log_decay, cotangent,
):
    def turn(a):
        return jnp.swapaxes(a, -1, -2)

    def by_head(a):
        return turn(a).reshape(KVH, HD, TOK)

    grad_q, grad_k, grad_v, grad_meta, grad_input, grad_bm, grad_cm = hand_out(
        run_layer(
            windows, by_head(key_vectors[0]), by_head(value_vectors[0]), turn(ssm_input[0]), turn(cotangent[0]),
            turn(queries[0]), turn(input_map[0]), turn(output_map[0]), log_decay.transpose(2, 0, 1),
            by_head(meta_keys), by_head(meta_values),
        )
    )
    return (
        turn(grad_q)[None], turn(grad_k)[None], turn(grad_v)[None], grad_meta.transpose(1, 2, 0),
        turn(grad_input)[None], turn(grad_bm)[None], turn(grad_cm)[None],
    )


def solution(mesh):
    seq = P("dp", "ctx", None)
    return jax.shard_map(
        local,
        mesh=mesh,
        in_specs=(seq, seq, seq, P(), P(), P(), seq, seq, seq, seq, seq),
        out_specs=(seq, seq, seq, P(None, "dp", "ctx"), seq, seq, seq),
        check_vma=False,
    )
```

time: 690 us -> 85.8 us (0.12); the launches traced: 680 us -> 85.6 us
  blocking collectives: 344 us -> 0 us
  other arithmetic: 150 us -> 0 us
  Pallas kernels: 0 us -> 85 us
  matrix products: 73.1 us -> 0 us
  starting transfers between devices: 51.8 us -> 0 us
  waiting for transfers between devices: 23.5 us -> 0 us
  between operations: 17.3 us -> 0.64 us
  local copies, waits for them, and re-layouts: 14.7 us -> 0 us
    unnamed x1 -> x0, blocking collectives: 255 us -> none
    select_n x128 -> x0, other arithmetic: 134 us -> none  [turn(): return jax.tree.map(lambda a, b: jnp.where(reached, a, b), new, before)]
    all_gather x1 -> x0, blocking collectives: 88.3 us -> none  [entering(): everything = jax.tree.map(lambda part: lax.all_gather(part, axis), shard)]
    pallas_call x0 -> x2, Pallas kernels: none -> 85 us  [the longest x1 82.9 us: run_layer(): pl.pallas_call(layer_kernel, out_shape=tuple((jax.ShapeDtypeStruct(s, t)...]
    dot_general x70 -> x0, matrix products: 73.1 us -> none  [the longest x5 11.3 us: head_terms(): jnp.einsum('gqe,ke->gqk', grad_h, value_h, preferred_element_type=jnp.flo...]
    ppermute x16 -> x0, starting transfers between devices: 51.7 us -> none  [from_behind(): return lax.ppermute(shard, axis, pairs)]
    ppermute x16 -> x0, waiting for transfers between devices: 23.5 us -> none  [from_behind(): return lax.ppermute(shard, axis, pairs)]
  transfers between devices with their start and end apart: 19 -> 0, of which waited for: 4 -> 0; matrix products, arithmetic and copies ran while one was open for 12% -> 0% of each run, Pallas kernels for 0% -> 0%
where the time goes in v2:
time: 85.8 us; the launch traced here: 85.6 us
  Pallas kernels  85 us (99%)
    pallas_call x1, Pallas kernels, run_layer(): pl.pallas_call(layer_kernel, out_shape=tuple((jax.ShapeDtypeStruct(s, t)...  82.9 us
    pallas_call x1, Pallas kernels, hand_out(): pl.pallas_call(hand_out_kernel, out_shape=tuple((jax.ShapeDtypeStruct(s,...  2.1 us

profile of v2, /device:TPU:1, one launch (start us, length us, event | category | flops | bytes accessed | tf_op | source)
XLA Modules:
  0.0 85.6 jit_solution(11466315518012264927)
XLA Ops:
  0.6 82.9 %layer_grads.1 = (bf16[1600,128]{1,0:T(8,128)(2,1)}, bf16[320,128]{1,0:T(8,128)(2,1)}, bf16[320,128]{1,0:T(8,128)(2,1)}, f32[5,2,16]{2,1,0:T(2,128)}, bf16[1600,...) custom-call(s32[25]{0:T(128)} %wins.1, bf16[5,64,128]{2,1,0:T(8,128)(2,1)} %bitcast.54, ...), custom_call_target="tpu_custom_call" | custom-call | tf_op jit(solution)/shard_map/layer_grads/pallas_call | solution.py:436
  83.5 2.1 %hand_out.1 = (bf16[1600,128]{1,0:T(8,128)(2,1)}, bf16[320,128]{1,0:T(8,128)(2,1)}, bf16[320,128]{1,0:T(8,128)(2,1)}, f32[5,2,16]{2,1,0:T(2,128)}, bf16[1600,128...) custom-call(bf16[1600,128]{1,0:T(8,128)(2,1)} %get-tuple-element.21.refs_0_, ...), custom_call_target="tpu_custom_call" | custom-call | tf_op jit(solution)/shard_map/hand_out/pallas_call | solution.py:485

commit v3 on v2

--- a/solution.py
+++ b/solution.py
@@ -48,7 +48,7 @@
     gq, gk, gv, gm, gin, gbm, gcm,
     x, g, q, bm, cm, ldv, ldp, xt, gt, loc, win, metas, qg, dist, ps, pieces, own, sink,
     stq, r1, d0, d1, s2, r2, d2s, d2, s3, r3, d3s, d3, ib, ob, inc, adj,
-    rc, ry, rz, sc, sb, sy, sa, k0, a0, k1, a1, k2, a2, k3, a3, k4, a4, k5,
+    rc, ry, rz, sc, sb, sy, sa, k0, a0, k1, a2, k4, a4, k5,
     in_sem, kv_send, kv_recv, c_send, c_recv, q1_send, q1_recv, q2_send, q2_recv, q3_send, q3_recv,
     q4_send, q4_recv, e_send, e_recv, t_send, t_recv, m_send, m_recv,
 ):
@@ -59,18 +59,20 @@
     base = i - c
     ahead2, ahead4 = (i + 2) % 64, (i + 4) % 64
     back2, back4 = (i + 62) % 64, (i + 60) % 64
+    along_z = [(z + k) % 16 for k in range(1, 16)]
     group = [base + (c + k) % 4 for k in (1, 2, 3)]
     near = [(zh * 4 + (zl + k) % 4) * 4 + c for k in (1, 2, 3)]
     far = [(((zh + k) % 4) * 4 + zl) * 4 + c for k in (1, 2, 3)]
     mate = base + (c + 1 - 2 * core)
     across = base + (c + 2) % 4
-    along_x = [(yl * 4 + (xx + k) % 4, i) for k in (1, 2, 3)]
-    other = (1 - yl) * 4 + xx
-    along_y = [(dp, across), (other, i), (other, across)]
+    diag = across + 1 - 2 * core
+    along_xy = [
+        (((yl + a) % 2) * 4 + (xx + k) % 4, base + ((yh + b) % 2) * 2 + core)
+        for k in range(4) for a in range(2) for b in range(2) if k + a + b > 0
+    ]
 
     barrier = pltpu.get_barrier_semaphore()
-    here = [(dp, to) for to in group + near + far + [ahead2, ahead4, back2, back4]]
-    for to in here + along_x + along_y[1:]:
+    for to in [(dp, 4 * there + c) for there in along_z] + along_xy + [(dp, o) for o in (mate, diag, ahead2, back2)]:
         pl.semaphore_signal(barrier, inc=1, device_id=to, device_id_type=MESH)
 
     def fetch(n, src, dst):
@@ -118,19 +120,40 @@
     d0[...] = jnp.broadcast_to(jnp.exp(run[TOK - 1 : TOK, :]), (8, 32))
     for copy in first_in:
         copy.wait()
-    pl.semaphore_wait(barrier, 18)
-
-    def mate_copy(d, n):
-        return pair(win.at[d], win.at[(d + core * 9 + (1 - core)) % 10], c_send, c_recv, n, (dp, mate))
-
-    step_a = pair(win.at[0], win.at[4], kv_send, kv_recv, 0, (dp, ahead4))
-    step_y = pair(win.at[0], win.at[2], kv_send, kv_recv, 1, (dp, ahead2))
-    step_b = pair(win.at[2], win.at[6], kv_send, kv_recv, 2, (dp, ahead4))
-    step_c = pair(win.at[4], win.at[8], kv_send, kv_recv, 3, (dp, ahead4))
-    mates = [mate_copy(d, n) for n, d in enumerate((0, 4, 2, 8, 6))]
-    step_y.start()
-    step_a.start()
-    mates[0].start()
+    pl.semaphore_wait(barrier, 34)
+
+    def kv_copies(n, lo, hi):
+        def step(src, dst, m, to):
+            return pair(win.at[src, lo:hi], win.at[dst, lo:hi], kv_send, kv_recv, 4 * n + m, (dp, to))
+
+        def to_mate(d, m):
+            there = (d + core * 9 + (1 - core)) % 10
+            return pair(win.at[d, lo:hi], win.at[there, lo:hi], c_send, c_recv, 5 * n + m, (dp, mate))
+
+        steps = (step(0, 2, 0, ahead2), step(0, 4, 1, ahead4), step(2, 6, 2, ahead4), step(4, 8, 3, ahead4))
+        return steps, [to_mate(d, m) for m, d in enumerate((0, 2, 4, 6, 8))]
+
+    halves = [kv_copies(0, 0, 2), kv_copies(1, 2, KVH)]
+    for steps, mates in halves:
+        steps[0].start()
+        steps[1].start()
+        mates[0].start()
+
+    def forward(n):
+        steps, mates = halves[n]
+        steps[0].wait_recv()
+        steps[2].start()
+        mates[1].start()
+        steps[1].wait_recv()
+        steps[3].start()
+        mates[2].start()
+
+    def finish(n):
+        steps, mates = halves[n]
+        steps[2].wait_recv()
+        mates[3].start()
+        steps[3].wait_recv()
+        mates[4].start()
 
     q1 = []
     for n, k in enumerate((1, 2, 3)):
@@ -153,14 +176,9 @@
     gram = jnp.zeros((TOK, TOK), F32)
     for h in range(0, 10):
         gram = local_head(h, gram)
-    step_a.wait_recv()
-    step_c.start()
-    mates[1].start()
-    for h in range(10, 18):
+    forward(0)
+    for h in range(10, 16):
         gram = local_head(h, gram)
-    step_y.wait_recv()
-    step_b.start()
-    mates[2].start()
 
     row, lane = iota((32, 512), 0), iota((32, 512), 1)
     onehot = ((row == 7 * c + lane // HD) & (lane < QL)).astype(BF)
@@ -236,8 +254,9 @@
         ob[c] = ib[c]
 
     scan_second()
-    for h in range(18, HEADS):
+    for h in range(16, HEADS):
         gram = local_head(h, gram)
+    forward(1)
     gram = gram.astype(BF)
     gbm[...] = dot(cm[...], gram)
     gcm[...] = dot(bm[...], gram, NT)
@@ -261,11 +280,8 @@
         dist[:, TOK * (d + 1) : TOK * (d + 2)] = jnp.where(i >= d, behind_by + TOK * d, never)
     pieces[9] = jnp.zeros((KVH, TOK, TOK), BF)
 
-    step_c.wait_recv()
-    mates[3].start()
-    step_b.wait_recv()
-    mates[4].start()
-    for copy in mates:
+    finish(0)
+    for copy in halves[0][1]:
         copy.wait_recv()
 
     def keys_of(k):
@@ -290,9 +306,15 @@
 
         @pl.when(k == 0)
         def _():
+            finish(1)
             scan_third()
 
-        @pl.when(k == 3)
+        @pl.when(k == 1)
+        def _():
+            for copy in halves[1][1]:
+                copy.wait_recv()
+
+        @pl.when(k == 4)
         def _():
             scan_fourth()
 
@@ -300,12 +322,21 @@
 
     lax.fori_loop(0, KVH, probs_of, 0)
 
+    held = (20 * z) // 64 - (20 * z) // 256
     m0 = pair(sink.at[1 - core], k0, m_send, m_recv, 0, (dp, mate))
-    m1 = [pair(a0.at[(xx + k) % 4], k1.at[n], m_send, m_recv, 1 + n, along_x[n]) for n, k in enumerate((1, 2, 3))]
-    m2 = [pair(a1.at[yl if n == 0 else 1 - yl], k2.at[n], m_send, m_recv, 4 + n, along_y[n]) for n in range(3)]
-    m3 = [pair(a2, k3.at[n], m_send, m_recv, 7 + n, (dp, near[n])) for n in range(3)]
-    m4 = [pair(a3, k4.at[n], m_send, m_recv, 10 + n, (dp, far[n])) for n in range(3)]
-    m5 = pair(a4, k5, m_send, m_recv, 13, (dp, mate))
+    m1 = [
+        pair(a0.at[to[0] % 4, to[0] // 4], k1.at[n], m_send, m_recv, 1 + n, to) for n, to in enumerate(along_xy)
+    ]
+    m2 = [
+        pair(a2.at[pl.ds((20 * to) // 64 - (20 * to) // 256, 2)], k4.at[n], m_send, m_recv, 16 + n, (dp, 4 * to + c))
+        for n, to in enumerate(along_z)
+    ]
+    m3 = pair(a4, k5, m_send, m_recv, 31, (dp, mate))
+
+    def total(own_part, parts):
+        for n in range(15):
+            own_part = own_part + parts[n]
+        return own_part
 
     def pass_on(arrived, result, value, following):
         for copy in arrived:
@@ -315,6 +346,43 @@
             copy.start()
 
     m0.start()
+
+    parts = ((0, 3), (3, KVH))
+    order = (6, 8, 2, 4, 0)
+    gives = [
+        [
+            pair(
+                pieces.at[(d + core + 9 * (1 - core)) % 10, lo:hi], rc.at[m, lo:hi],
+                e_send, e_recv, 5 * n + m, (dp, mate),
+            )
+            for m, d in enumerate(order)
+        ]
+        for n, (lo, hi) in enumerate(parts)
+    ]
+    backs = [
+        [
+            pair(src.at[lo:hi], dst.at[lo:hi], t_send, t_recv, 4 * n + m, (dp, to))
+            for m, (src, dst, to) in enumerate(
+                ((sb, rz.at[1], back4), (sc, rz.at[0], back4), (sy, ry, back2), (sa, rz.at[2], back4))
+            )
+        ]
+        for n, (lo, hi) in enumerate(parts)
+    ]
+
+    def send_far(n):
+        lo, hi = parts[n]
+        for m, out in ((0, sb), (1, sc)):
+            gives[n][m].wait_recv()
+            out[lo:hi] = (pieces[order[m], lo:hi].astype(F32) + rc[m, lo:hi].astype(F32)).astype(BF)
+            backs[n][m].start()
+
+    def send_near(n, m, out, arrived):
+        lo, hi = parts[n]
+        gives[n][m].wait_recv()
+        backs[n][m - 2].wait_recv()
+        part = pieces[order[m], lo:hi].astype(F32) + rc[m, lo:hi].astype(F32)
+        out[lo:hi] = (part + rz[arrived, lo:hi].astype(F32)).astype(BF)
+        backs[n][m].start()
 
     def grads_of(k, carry):
         kv = keys_of(k)
@@ -333,33 +401,26 @@
 
         @pl.when(k == 2)
         def _():
-            pass_on(m1, a1, lambda: a0[xx] + k1[0] + k1[1] + k1[2], m2)
+            for copy in gives[0]:
+                copy.start()
+
+        @pl.when(k == 3)
+        def _():
+            send_far(0)
 
         @pl.when(k == 4)
         def _():
-            pass_on(m2, a2, lambda: a1[yl] + k2[0] + k2[1] + k2[2], m3)
+            for copy in gives[1]:
+                copy.start()
+            pass_on(m1, a2, lambda: total(a0[xx, yl], k1), m2)
 
         return carry
 
     lax.fori_loop(0, KVH, grads_of, 0)
 
-    give = [
-        pair(pieces.at[(d + core + 9 * (1 - core)) % 10], rc.at[n], e_send, e_recv, n, (dp, mate))
-        for n, d in enumerate((8, 6, 2, 4, 0))
-    ]
-    for copy in give:
-        copy.start()
-    back_c = pair(sc, rz.at[0], t_send, t_recv, 0, (dp, back4))
-    back_b = pair(sb, rz.at[1], t_send, t_recv, 1, (dp, back4))
-    back_y = pair(sy, ry, t_send, t_recv, 2, (dp, back2))
-    back_a = pair(sa, rz.at[2], t_send, t_recv, 3, (dp, back4))
-    give[1].wait_recv()
-    sb[...] = (pieces[6].astype(F32) + rc[1].astype(F32)).astype(BF)
-    back_b.start()
-    give[0].wait_recv()
-    sc[...] = (pieces[8].astype(F32) + rc[0].astype(F32)).astype(BF)
-    back_c.start()
-    pass_on(m3, a3, lambda: a2[...] + k3[0] + k3[1] + k3[2], m4)
+    send_far(1)
+    send_near(0, 2, sy, 1)
+    send_near(0, 3, sa, 0)
 
     for copy in q4:
         copy.wait_recv()
@@ -371,16 +432,8 @@
     gbm[...] = gbm[...] + dot(adj_h, xt[...])
     gcm[...] = gcm[...] + dot(inc_h, gt[...])
 
-    for copy in give[2:]:
-        copy.wait_recv()
-    sum_y = pieces[2].astype(F32) + rc[2].astype(F32)
-    back_b.wait_recv()
-    sy[...] = (sum_y + rz[1].astype(F32)).astype(BF)
-    back_y.start()
-    sum_a = pieces[4].astype(F32) + rc[3].astype(F32)
-    back_c.wait_recv()
-    sa[...] = (sum_a + rz[0].astype(F32)).astype(BF)
-    back_a.start()
+    send_near(1, 2, sy, 1)
+    send_near(1, 3, sa, 0)
 
     carried = dot(adj_h, bm[...], TN)
     tail = jnp.exp(end - run_t)
@@ -388,20 +441,22 @@
         f = slice(HD * h, HD * h + HD)
         gin[f, :] = (loc[f, :] + tail[h : h + 1, :] * carried[f]).astype(BF)
 
-    pass_on(m4, a4, lambda: a3[...] + k4[0] + k4[1] + k4[2], [m5])
-    back_y.wait_recv()
-    back_a.wait_recv()
+    pass_on(m2, a4, lambda: total(a2[pl.ds(held, 2)], k4), [m3])
+    for n in range(2):
+        gives[n][4].wait_recv()
+        backs[n][2].wait_recv()
+        backs[n][3].wait_recv()
     for k in range(KVH):
         mine = own[k] + rc[4, k].astype(F32) + ry[k].astype(F32) + rz[2, k].astype(F32)
         gk[HD * k : HD * k + HD, :] = mine[:HD].astype(BF)
         gv[HD * k : HD * k + HD, :] = mine[HD:].astype(BF)
 
-    m5.wait_recv()
+    m3.wait_recv()
     row, lane = iota((16, TOK), 0), iota((16, TOK), 1)
     first = jnp.zeros((16, 8), F32)
     second = jnp.zeros((16, 8), F32)
-    for k in range(KVH):
-        feature = 5 * i + row % 8 - HD * k
+    for k in range(2):
+        feature = 5 * i + row % 8 - HD * (held + k)
         pick = (row % 8 < 5) & (feature >= 0) & (feature < HD) & (lane == feature + HD * (row // 8))
         pick = pick.astype(BF)
         for part in split3(a4[k]):
@@ -415,10 +470,11 @@
             gm[j, w : w + 1, 0:8] = left[8 * w + j : 8 * w + j + 1]
             gm[j, w : w + 1, 8:16] = right[8 * w + j : 8 * w + j + 1]
 
-    for copy in [step_a, step_y, step_b, step_c] + mates + q1 + q2 + q3 + q4:
+    for copy in q1 + q2 + q3 + q4 + [m0, m3] + m1 + m2:
         copy.wait_send()
-    for copy in give + [back_a, back_b, back_c, back_y, m0, m5] + m1 + m2 + m3 + m4:
-        copy.wait_send()
+    for n in range(2):
+        for copy in list(halves[n][0]) + halves[n][1] + gives[n] + backs[n]:
+            copy.wait_send()
 
 
 OUTS = (
@@ -452,14 +508,10 @@
             vm((5,) + block, BF), vm(block, BF), vm((3,) + block, BF),
             vm(block, BF), vm(block, BF), vm(block, BF), vm(block, BF),
             vm((4, 2) + part, F32), vm((4, 2) + part, F32),
-            vm((3, 2) + part, F32), vm((2,) + part, F32),
-            vm((3,) + part, F32), vm(part, F32),
-            vm((3,) + part, F32), vm(part, F32),
-            vm((3,) + part, F32), vm(part, F32),
-            vm(part, F32),
-            dma((10,)), dma((4,)), dma((4,)), dma((5,)), dma((5,)),
+            vm((15,) + part, F32), vm(part, F32), vm((15, 2, 8, TOK), F32), vm((2, 8, TOK), F32), vm((2, 8, TOK), F32),
+            dma((10,)), dma((8,)), dma((8,)), dma((10,)), dma((10,)),
             dma((6,)), dma((6,)), dma((6,)), dma((6,)), dma((6,)), dma((6,)), dma((3,)), dma((3,)),
-            dma((5,)), dma((5,)), dma((4,)), dma((4,)), dma((14,)), dma((14,)),
+            dma((10,)), dma((10,)), dma((8,)), dma((8,)), dma((32,)), dma((32,)),
         ],
         compiler_params=pltpu.CompilerParams(
             collective_id=0, has_side_effects=True, vmem_limit_bytes=56 * 1024 * 1024

time: 85.8 us -> 78.6 us (0.916)
  Pallas kernels: 85 us -> 77.8 us
    pallas_call x1, Pallas kernels: 82.9 us -> 75.7 us  [run_layer(): pl.pallas_call(layer_kernel, out_shape=tuple((jax.ShapeDtypeStruct(s, t)...]
where the time goes in v3:
time: 78.6 us; the launch traced here: 78.5 us
  Pallas kernels  77.8 us (99%)
    pallas_call x1, Pallas kernels, run_layer(): pl.pallas_call(layer_kernel, out_shape=tuple((jax.ShapeDtypeStruct(s, t)...  75.7 us
    pallas_call x1, Pallas kernels, hand_out(): pl.pallas_call(hand_out_kernel, out_shape=tuple((jax.ShapeDtypeStruct(s,...  2.1 us

profile of v3, /device:TPU:1, one launch (start us, length us, event | category | flops | bytes accessed | tf_op | source)
XLA Modules:
  0.0 78.5 jit_solution(13313184092594924232)
XLA Ops:
  0.6 75.7 %layer_grads.1 = (bf16[1600,128]{1,0:T(8,128)(2,1)}, bf16[320,128]{1,0:T(8,128)(2,1)}, bf16[320,128]{1,0:T(8,128)(2,1)}, f32[5,2,16]{2,1,0:T(2,128)}, bf16[1600,...) custom-call(s32[25]{0:T(128)} %wins.1, bf16[5,64,128]{2,1,0:T(8,128)(2,1)} %bitcast.54, ...), custom_call_target="tpu_custom_call" | custom-call | tf_op jit(solution)/shard_map/layer_grads/pallas_call | solution.py:492
  76.4 2.1 %hand_out.1 = (bf16[1600,128]{1,0:T(8,128)(2,1)}, bf16[320,128]{1,0:T(8,128)(2,1)}, bf16[320,128]{1,0:T(8,128)(2,1)}, f32[5,2,16]{2,1,0:T(2,128)}, bf16[1600,128...) custom-call(bf16[1600,128]{1,0:T(8,128)(2,1)} %get-tuple-element.21.refs_0_, ...), custom_call_target="tpu_custom_call" | custom-call | tf_op jit(solution)/shard_map/hand_out/pallas_call | solution.py:537

commit v4 on v3

--- a/solution.py
+++ b/solution.py
@@ -50,7 +50,7 @@
     stq, r1, d0, d1, s2, r2, d2s, d2, s3, r3, d3s, d3, ib, ob, inc, adj,
     rc, ry, rz, sc, sb, sy, sa, k0, a0, k1, a2, k4, a4, k5,
     in_sem, kv_send, kv_recv, c_send, c_recv, q1_send, q1_recv, q2_send, q2_recv, q3_send, q3_recv,
-    q4_send, q4_recv, e_send, e_recv, t_send, t_recv, m_send, m_recv,
+    q4_send, q4_recv, e_send, e_recv, t_send, t_recv, m_send, m_recv, vouch,
 ):
     dp, i, core, yh, z = places()
     c = i % 4
@@ -72,7 +72,8 @@
     ]
 
     barrier = pltpu.get_barrier_semaphore()
-    for to in [(dp, 4 * there + c) for there in along_z] + along_xy + [(dp, o) for o in (mate, diag, ahead2, back2)]:
+    close = [(z + k) % 16 for k in (1, 2, 3, 4, 12, 13, 14, 15)]
+    for to in [(dp, 4 * there + c) for there in close] + along_xy + [(dp, o) for o in (mate, diag, ahead2, back2)]:
         pl.semaphore_signal(barrier, inc=1, device_id=to, device_id_type=MESH)
 
     def fetch(n, src, dst):
@@ -120,7 +121,11 @@
     d0[...] = jnp.broadcast_to(jnp.exp(run[TOK - 1 : TOK, :]), (8, 32))
     for copy in first_in:
         copy.wait()
-    pl.semaphore_wait(barrier, 34)
+    pl.semaphore_wait(barrier, 27)
+    for k in (4, 12):
+        pl.semaphore_signal(
+            vouch, inc=1, device_id=(dp, 4 * ((z + k) % 16) + c), device_id_type=MESH
+        )
 
     def kv_copies(n, lo, hi):
         def step(src, dst, m, to):
@@ -222,6 +227,7 @@
     def scan_third():
         for copy in q2:
             copy.wait_recv()
+        pl.semaphore_wait(vouch, 2)
         s3[0], s3[1] = sums(expand(d2), r2)
         d3s[...] = d2[0] * d2[1] * d2[2] * d2[3]
         for copy in q3:
@@ -256,6 +262,7 @@
     scan_second()
     for h in range(16, HEADS):
         gram = local_head(h, gram)
+    finish(0)
     forward(1)
     gram = gram.astype(BF)
     gbm[...] = dot(cm[...], gram)
@@ -280,7 +287,6 @@
         dist[:, TOK * (d + 1) : TOK * (d + 2)] = jnp.where(i >= d, behind_by + TOK * d, never)
     pieces[9] = jnp.zeros((KVH, TOK, TOK), BF)
 
-    finish(0)
     for copy in halves[0][1]:
         copy.wait_recv()
 
@@ -347,7 +353,7 @@
 
     m0.start()
 
-    parts = ((0, 3), (3, KVH))
+    parts = ((0, 2), (2, 4), (4, KVH))
     order = (6, 8, 2, 4, 0)
     gives = [
         [
@@ -399,28 +405,35 @@
         def _():
             pass_on([m0], a0, lambda: sink[core] + k0[...], m1)
 
-        @pl.when(k == 2)
+        @pl.when(k == 1)
         def _():
             for copy in gives[0]:
                 copy.start()
 
+        @pl.when(k == 2)
+        def _():
+            send_far(0)
+
         @pl.when(k == 3)
-        def _():
-            send_far(0)
-
-        @pl.when(k == 4)
         def _():
             for copy in gives[1]:
                 copy.start()
+
+        @pl.when(k == 4)
+        def _():
+            for copy in gives[2]:
+                copy.start()
+            send_far(1)
             pass_on(m1, a2, lambda: total(a0[xx, yl], k1), m2)
 
         return carry
 
     lax.fori_loop(0, KVH, grads_of, 0)
 
-    send_far(1)
-    send_near(0, 2, sy, 1)
-    send_near(0, 3, sa, 0)
+    send_far(2)
+    for n in (0, 1):
+        send_near(n, 2, sy, 1)
+        send_near(n, 3, sa, 0)
 
     for copy in q4:
         copy.wait_recv()
@@ -432,8 +445,8 @@
     gbm[...] = gbm[...] + dot(adj_h, xt[...])
     gcm[...] = gcm[...] + dot(inc_h, gt[...])
 
-    send_near(1, 2, sy, 1)
-    send_near(1, 3, sa, 0)
+    send_near(2, 2, sy, 1)
+    send_near(2, 3, sa, 0)
 
     carried = dot(adj_h, bm[...], TN)
     tail = jnp.exp(end - run_t)
@@ -442,7 +455,7 @@
         gin[f, :] = (loc[f, :] + tail[h : h + 1, :] * carried[f]).astype(BF)
 
     pass_on(m2, a4, lambda: total(a2[pl.ds(held, 2)], k4), [m3])
-    for n in range(2):
+    for n in range(3):
         gives[n][4].wait_recv()
         backs[n][2].wait_recv()
         backs[n][3].wait_recv()
@@ -472,9 +485,11 @@
 
     for copy in q1 + q2 + q3 + q4 + [m0, m3] + m1 + m2:
         copy.wait_send()
-    for n in range(2):
-        for copy in list(halves[n][0]) + halves[n][1] + gives[n] + backs[n]:
+    for steps, mates in halves:
+        for copy in list(steps) + mates:
             copy.wait_send()
+    for copy in sum(gives, []) + sum(backs, []):
+        copy.wait_send()
 
 
 OUTS = (
@@ -511,7 +526,7 @@
             vm((15,) + part, F32), vm(part, F32), vm((15, 2, 8, TOK), F32), vm((2, 8, TOK), F32), vm((2, 8, TOK), F32),
             dma((10,)), dma((8,)), dma((8,)), dma((10,)), dma((10,)),
             dma((6,)), dma((6,)), dma((6,)), dma((6,)), dma((6,)), dma((6,)), dma((3,)), dma((3,)),
-            dma((10,)), dma((10,)), dma((8,)), dma((8,)), dma((32,)), dma((32,)),
+            dma((15,)), dma((15,)), dma((12,)), dma((12,)), dma((32,)), dma((32,)), pltpu.SemaphoreType.REGULAR,
         ],
         compiler_params=pltpu.CompilerParams(
             collective_id=0, has_side_effects=True, vmem_limit_bytes=56 * 1024 * 1024

time: 78.6 us -> 74 us (0.941)
  Pallas kernels: 77.8 us -> 73.2 us
    pallas_call x1, Pallas kernels: 75.7 us -> 71.1 us  [run_layer(): pl.pallas_call(layer_kernel, out_shape=tuple((jax.ShapeDtypeStruct(s, t)...]
where the time goes in v4:
time: 74 us; the launch traced here: 73.8 us
  Pallas kernels  73.2 us (99%)
    pallas_call x1, Pallas kernels, run_layer(): pl.pallas_call(layer_kernel, out_shape=tuple((jax.ShapeDtypeStruct(s, t)...  71.1 us
    pallas_call x1, Pallas kernels, hand_out(): pl.pallas_call(hand_out_kernel, out_shape=tuple((jax.ShapeDtypeStruct(s,...  2.1 us

profile of v4, /device:TPU:1, one launch (start us, length us, event | category | flops | bytes accessed | tf_op | source)
XLA Modules:
  0.0 73.8 jit_solution(9030603477590427827)
XLA Ops:
  0.6 71.1 %layer_grads.1 = (bf16[1600,128]{1,0:T(8,128)(2,1)}, bf16[320,128]{1,0:T(8,128)(2,1)}, bf16[320,128]{1,0:T(8,128)(2,1)}, f32[5,2,16]{2,1,0:T(2,128)}, bf16[1600,...) custom-call(s32[25]{0:T(128)} %wins.1, bf16[5,64,128]{2,1,0:T(8,128)(2,1)} %bitcast.54, ...), custom_call_target="tpu_custom_call" | custom-call | tf_op jit(solution)/shard_map/layer_grads/pallas_call | solution.py:507
  71.7 2.1 %hand_out.1 = (bf16[1600,128]{1,0:T(8,128)(2,1)}, bf16[320,128]{1,0:T(8,128)(2,1)}, bf16[320,128]{1,0:T(8,128)(2,1)}, f32[5,2,16]{2,1,0:T(2,128)}, bf16[1600,128...) custom-call(bf16[1600,128]{1,0:T(8,128)(2,1)} %get-tuple-element.21.refs_0_, ...), custom_call_target="tpu_custom_call" | custom-call | tf_op jit(solution)/shard_map/hand_out/pallas_call | solution.py:552

commit v5 on v4

--- a/solution.py
+++ b/solution.py
@@ -93,6 +93,47 @@
             device_id=to, device_id_type=MESH,
         )
 
+    for copy in first_in:
+        copy.wait()
+    pl.semaphore_wait(barrier, 27)
+    for k in (4, 12):
+        pl.semaphore_signal(
+            vouch, inc=1, device_id=(dp, 4 * ((z + k) % 16) + c), device_id_type=MESH
+        )
+
+    def kv_copies(n, lo, hi):
+        def step(src, dst, m, to):
+            return pair(win.at[src, lo:hi], win.at[dst, lo:hi], kv_send, kv_recv, 4 * n + m, (dp, to))
+
+        def to_mate(d, m):
+            there = (d + core * 9 + (1 - core)) % 10
+            return pair(win.at[d, lo:hi], win.at[there, lo:hi], c_send, c_recv, 5 * n + m, (dp, mate))
+
+        steps = (step(0, 2, 0, ahead2), step(0, 4, 1, ahead4), step(2, 6, 2, ahead4), step(4, 8, 3, ahead4))
+        return steps, [to_mate(d, m) for m, d in enumerate((0, 2, 4, 6, 8))]
+
+    halves = [kv_copies(0, 0, 2), kv_copies(1, 2, KVH)]
+    for steps, mates in halves:
+        steps[0].start()
+        steps[1].start()
+        mates[0].start()
+
+    def forward(n):
+        steps, mates = halves[n]
+        steps[0].wait_recv()
+        steps[2].start()
+        mates[1].start()
+        steps[1].wait_recv()
+        steps[3].start()
+        mates[2].start()
+
+    def finish(n):
+        steps, mates = halves[n]
+        steps[2].wait_recv()
+        mates[3].start()
+        steps[3].wait_recv()
+        mates[4].start()
+
     for copy in scan_in:
         copy.wait()
     rows, cols = iota((TOK, TOK), 0), iota((TOK, TOK), 1)
@@ -119,47 +160,6 @@
                 [terms[:, QL * p : QL * p + n], jnp.zeros((STATE, 512 - n), F32)], axis=1
             ).astype(BF)
     d0[...] = jnp.broadcast_to(jnp.exp(run[TOK - 1 : TOK, :]), (8, 32))
-    for copy in first_in:
-        copy.wait()
-    pl.semaphore_wait(barrier, 27)
-    for k in (4, 12):
-        pl.semaphore_signal(
-            vouch, inc=1, device_id=(dp, 4 * ((z + k) % 16) + c), device_id_type=MESH
-        )
-
-    def kv_copies(n, lo, hi):
-        def step(src, dst, m, to):
-            return pair(win.at[src, lo:hi], win.at[dst, lo:hi], kv_send, kv_recv, 4 * n + m, (dp, to))
-
-        def to_mate(d, m):
-            there = (d + core * 9 + (1 - core)) % 10
-            return pair(win.at[d, lo:hi], win.at[there, lo:hi], c_send, c_recv, 5 * n + m, (dp, mate))
-
-        steps = (step(0, 2, 0, ahead2), step(0, 4, 1, ahead4), step(2, 6, 2, ahead4), step(4, 8, 3, ahead4))
-        return steps, [to_mate(d, m) for m, d in enumerate((0, 2, 4, 6, 8))]
-
-    halves = [kv_copies(0, 0, 2), kv_copies(1, 2, KVH)]
-    for steps, mates in halves:
-        steps[0].start()
-        steps[1].start()
-        mates[0].start()
-
-    def forward(n):
-        steps, mates = halves[n]
-        steps[0].wait_recv()
-        steps[2].start()
-        mates[1].start()
-        steps[1].wait_recv()
-        steps[3].start()
-        mates[2].start()
-
-    def finish(n):
-        steps, mates = halves[n]
-        steps[2].wait_recv()
-        mates[3].start()
-        steps[3].wait_recv()
-        mates[4].start()
-
     q1 = []
     for n, k in enumerate((1, 2, 3)):
         q1.append(pair(stq.at[(c + k) % 4], r1.at[c], q1_send, q1_recv, n, (dp, group[n])))
@@ -179,11 +179,33 @@
         return gram + mix * dot(g[f, :], x[f, :], TN)
 
     gram = jnp.zeros((TOK, TOK), F32)
-    for h in range(0, 10):
+    for h in range(0, 8):
         gram = local_head(h, gram)
     forward(0)
-    for h in range(10, 16):
+
+    for copy in late_in:
+        copy.wait()
+    zeros = jnp.zeros((HD, TOK), BF)
+    for k in range(KVH):
+        for j in range(GROUP):
+            f = slice(HD * (GROUP * k + j), HD * (GROUP * k + j) + HD)
+            at = 2 * TOK * j
+            qg[k, 0:HD, at : at + TOK] = (q[f, :].astype(F32) * 0.125).astype(BF)
+            qg[k, 0:HD, at + TOK : at + 2 * TOK] = zeros
+            qg[k, HD : 2 * HD, at : at + TOK] = zeros
+            qg[k, HD : 2 * HD, at + TOK : at + 2 * TOK] = g[f, :]
+    behind_by = rows - cols
+    never = jnp.int32(1 << 20)
+    dist[:, 0:TOK] = jnp.zeros((TOK, TOK), jnp.int32)
+    dist[:, TOK : 2 * TOK] = jnp.where(behind_by >= 0, behind_by, never)
+    for d in range(1, 9):
+        dist[:, TOK * (d + 1) : TOK * (d + 2)] = jnp.where(i >= d, behind_by + TOK * d, never)
+    pieces[9] = jnp.zeros((KVH, TOK, TOK), BF)
+
+    for h in range(8, 14):
         gram = local_head(h, gram)
+    finish(0)
+    forward(1)
 
     row, lane = iota((32, 512), 0), iota((32, 512), 1)
     onehot = ((row == 7 * c + lane // HD) & (lane < QL)).astype(BF)
@@ -260,33 +282,6 @@
         ob[c] = ib[c]
 
     scan_second()
-    for h in range(16, HEADS):
-        gram = local_head(h, gram)
-    finish(0)
-    forward(1)
-    gram = gram.astype(BF)
-    gbm[...] = dot(cm[...], gram)
-    gcm[...] = dot(bm[...], gram, NT)
-
-    for copy in late_in:
-        copy.wait()
-    zeros = jnp.zeros((HD, TOK), BF)
-    for k in range(KVH):
-        for j in range(GROUP):
-            f = slice(HD * (GROUP * k + j), HD * (GROUP * k + j) + HD)
-            at = 2 * TOK * j
-            qg[k, 0:HD, at : at + TOK] = (q[f, :].astype(F32) * 0.125).astype(BF)
-            qg[k, 0:HD, at + TOK : at + 2 * TOK] = zeros
-            qg[k, HD : 2 * HD, at : at + TOK] = zeros
-            qg[k, HD : 2 * HD, at + TOK : at + 2 * TOK] = g[f, :]
-    behind_by = rows - cols
-    never = jnp.int32(1 << 20)
-    dist[:, 0:TOK] = jnp.zeros((TOK, TOK), jnp.int32)
-    dist[:, TOK : 2 * TOK] = jnp.where(behind_by >= 0, behind_by, never)
-    for d in range(1, 9):
-        dist[:, TOK * (d + 1) : TOK * (d + 2)] = jnp.where(i >= d, behind_by + TOK * d, never)
-    pieces[9] = jnp.zeros((KVH, TOK, TOK), BF)
-
     for copy in halves[0][1]:
         copy.wait_recv()
 
@@ -313,16 +308,12 @@
         @pl.when(k == 0)
         def _():
             finish(1)
-            scan_third()
 
         @pl.when(k == 1)
         def _():
             for copy in halves[1][1]:
                 copy.wait_recv()
-
-        @pl.when(k == 4)
-        def _():
-            scan_fourth()
+            scan_third()
 
         return carry
 
@@ -404,6 +395,7 @@
         @pl.when(k == 0)
         def _():
             pass_on([m0], a0, lambda: sink[core] + k0[...], m1)
+            scan_fourth()
 
         @pl.when(k == 1)
         def _():
@@ -442,12 +434,17 @@
         inc[:, QL * p : QL * p + n] = ob[p, 0].astype(F32)[:, :n]
         adj[:, QL * p : QL * p + n] = ob[p, 1].astype(F32)[:, :n]
     inc_h, adj_h = inc[...].astype(BF), adj[...].astype(BF)
-    gbm[...] = gbm[...] + dot(adj_h, xt[...])
-    gcm[...] = gcm[...] + dot(inc_h, gt[...])
+    grad_bm = dot(adj_h, xt[...])
+    grad_cm = dot(inc_h, gt[...])
 
     send_near(2, 2, sy, 1)
     send_near(2, 3, sa, 0)
 
+    for h in range(14, HEADS):
+        gram = local_head(h, gram)
+    gram = gram.astype(BF)
+    gbm[...] = grad_bm + dot(cm[...], gram)
+    gcm[...] = grad_cm + dot(bm[...], gram, NT)
     carried = dot(adj_h, bm[...], TN)
     tail = jnp.exp(end - run_t)
     for h in range(HEADS):

time: 74 us -> 74.6 us (level)
  no operation moved by 1% of the time
where the time goes in v5:
time: 74.6 us; the launch traced here: 74.4 us
  Pallas kernels  73.8 us (99%)
    pallas_call x1, Pallas kernels, run_layer(): pl.pallas_call(layer_kernel, out_shape=tuple((jax.ShapeDtypeStruct(s, t)...  71.7 us
    pallas_call x1, Pallas kernels, hand_out(): pl.pallas_call(hand_out_kernel, out_shape=tuple((jax.ShapeDtypeStruct(s,...  2.1 us

profile of v5, /device:TPU:1, one launch (start us, length us, event | category | flops | bytes accessed | tf_op | source)
XLA Modules:
  0.0 74.4 jit_solution(16998791579101588322)
XLA Ops:
  0.6 71.7 %layer_grads.1 = (bf16[1600,128]{1,0:T(8,128)(2,1)}, bf16[320,128]{1,0:T(8,128)(2,1)}, bf16[320,128]{1,0:T(8,128)(2,1)}, f32[5,2,16]{2,1,0:T(2,128)}, bf16[1600,...) custom-call(s32[25]{0:T(128)} %wins.1, bf16[5,64,128]{2,1,0:T(8,128)(2,1)} %bitcast.54, ...), custom_call_target="tpu_custom_call" | custom-call | tf_op jit(solution)/shard_map/layer_grads/pallas_call | solution.py:504
  72.3 2.1 %hand_out.1 = (bf16[1600,128]{1,0:T(8,128)(2,1)}, bf16[320,128]{1,0:T(8,128)(2,1)}, bf16[320,128]{1,0:T(8,128)(2,1)}, f32[5,2,16]{2,1,0:T(2,128)}, bf16[1600,128...) custom-call(bf16[1600,128]{1,0:T(8,128)(2,1)} %get-tuple-element.21.refs_0_, ...), custom_call_target="tpu_custom_call" | custom-call | tf_op jit(solution)/shard_map/hand_out/pallas_call | solution.py:549

commit v6 on v5

--- a/solution.py
+++ b/solution.py
@@ -416,16 +416,17 @@
             for copy in gives[2]:
                 copy.start()
             send_far(1)
+            send_near(0, 2, sy, 1)
+            send_near(0, 3, sa, 0)
+            send_far(2)
             pass_on(m1, a2, lambda: total(a0[xx, yl], k1), m2)
 
         return carry
 
     lax.fori_loop(0, KVH, grads_of, 0)
 
-    send_far(2)
-    for n in (0, 1):
-        send_near(n, 2, sy, 1)
-        send_near(n, 3, sa, 0)
+    send_near(1, 2, sy, 1)
+    send_near(1, 3, sa, 0)
 
     for copy in q4:
         copy.wait_recv()

time: 74.6 us -> 73 us (0.979)
  Pallas kernels: 73.8 us -> 72.2 us
    pallas_call x1, Pallas kernels: 71.7 us -> 70.1 us  [run_layer(): pl.pallas_call(layer_kernel, out_shape=tuple((jax.ShapeDtypeStruct(s, t)...]
where the time goes in v6:
time: 73 us; the launch traced here: 72.8 us
  Pallas kernels  72.2 us (99%)
    pallas_call x1, Pallas kernels, run_layer(): pl.pallas_call(layer_kernel, out_shape=tuple((jax.ShapeDtypeStruct(s, t)...  70.1 us
    pallas_call x1, Pallas kernels, hand_out(): pl.pallas_call(hand_out_kernel, out_shape=tuple((jax.ShapeDtypeStruct(s,...  2.1 us

profile of v6, /device:TPU:1, one launch (start us, length us, event | category | flops | bytes accessed | tf_op | source)
XLA Modules:
  0.0 72.8 jit_solution(8082382482399635644)
XLA Ops:
  0.6 70.1 %layer_grads.1 = (bf16[1600,128]{1,0:T(8,128)(2,1)}, bf16[320,128]{1,0:T(8,128)(2,1)}, bf16[320,128]{1,0:T(8,128)(2,1)}, f32[5,2,16]{2,1,0:T(2,128)}, bf16[1600,...) custom-call(s32[25]{0:T(128)} %wins.1, bf16[5,64,128]{2,1,0:T(8,128)(2,1)} %bitcast.54, ...), custom_call_target="tpu_custom_call" | custom-call | tf_op jit(solution)/shard_map/layer_grads/pallas_call | solution.py:505
  70.7 2.1 %hand_out.1 = (bf16[1600,128]{1,0:T(8,128)(2,1)}, bf16[320,128]{1,0:T(8,128)(2,1)}, bf16[320,128]{1,0:T(8,128)(2,1)}, f32[5,2,16]{2,1,0:T(2,128)}, bf16[1600,128...) custom-call(bf16[1600,128]{1,0:T(8,128)(2,1)} %get-tuple-element.21.refs_0_, ...), custom_call_target="tpu_custom_call" | custom-call | tf_op jit(solution)/shard_map/hand_out/pallas_call | solution.py:550

commit v7 on v6

--- a/solution.py
+++ b/solution.py
@@ -59,6 +59,7 @@
     base = i - c
     ahead2, ahead4 = (i + 2) % 64, (i + 4) % 64
     back2, back4 = (i + 62) % 64, (i + 60) % 64
+    ahead6, back6 = (i + 6) % 64, (i + 58) % 64
     along_z = [(z + k) % 16 for k in range(1, 16)]
     group = [base + (c + k) % 4 for k in (1, 2, 3)]
     near = [(zh * 4 + (zl + k) % 4) * 4 + c for k in (1, 2, 3)]
@@ -73,7 +74,7 @@
 
     barrier = pltpu.get_barrier_semaphore()
     close = [(z + k) % 16 for k in (1, 2, 3, 4, 12, 13, 14, 15)]
-    for to in [(dp, 4 * there + c) for there in close] + along_xy + [(dp, o) for o in (mate, diag, ahead2, back2)]:
+    for to in [(dp, 4 * there + c) for there in close] + along_xy + [(dp, o) for o in (mate, diag, ahead2, back2, ahead6, back6)]:
         pl.semaphore_signal(barrier, inc=1, device_id=to, device_id_type=MESH)
 
     def fetch(n, src, dst):
@@ -95,7 +96,7 @@
 
     for copy in first_in:
         copy.wait()
-    pl.semaphore_wait(barrier, 27)
+    pl.semaphore_wait(barrier, 29)
     for k in (4, 12):
         pl.semaphore_signal(
             vouch, inc=1, device_id=(dp, 4 * ((z + k) % 16) + c), device_id_type=MESH
@@ -109,10 +110,12 @@
             there = (d + core * 9 + (1 - core)) % 10
             return pair(win.at[d, lo:hi], win.at[there, lo:hi], c_send, c_recv, 5 * n + m, (dp, mate))
 
-        steps = (step(0, 2, 0, ahead2), step(0, 4, 1, ahead4), step(2, 6, 2, ahead4), step(4, 8, 3, ahead4))
+        third = step(0, 6, 2, ahead6) if n == 0 else step(2, 6, 2, ahead4)
+        steps = (step(0, 2, 0, ahead2), step(0, 4, 1, ahead4), third, step(4, 8, 3, ahead4))
         return steps, [to_mate(d, m) for m, d in enumerate((0, 2, 4, 6, 8))]
 
     halves = [kv_copies(0, 0, 2), kv_copies(1, 2, KVH)]
+    halves[0][0][2].start()
     for steps, mates in halves:
         steps[0].start()
         steps[1].start()
@@ -121,7 +124,8 @@
     def forward(n):
         steps, mates = halves[n]
         steps[0].wait_recv()
-        steps[2].start()
+        if n == 1:
+            steps[2].start()
         mates[1].start()
         steps[1].wait_recv()
         steps[3].start()
@@ -395,12 +399,12 @@
         @pl.when(k == 0)
         def _():
             pass_on([m0], a0, lambda: sink[core] + k0[...], m1)
-            scan_fourth()
 
         @pl.when(k == 1)
         def _():
             for copy in gives[0]:
                 copy.start()
+            scan_fourth()
 
         @pl.when(k == 2)
         def _():

time: 73 us -> 75.5 us (1.034)
  Pallas kernels: 72.2 us -> 74.6 us
    pallas_call x1, Pallas kernels: 70.1 us -> 72.5 us  [run_layer(): pl.pallas_call(layer_kernel, out_shape=tuple((jax.ShapeDtypeStruct(s, t)...]
where the time goes in v7:
time: 75.5 us; the launch traced here: 75.3 us
  Pallas kernels  74.6 us (99%)
    pallas_call x1, Pallas kernels, run_layer(): pl.pallas_call(layer_kernel, out_shape=tuple((jax.ShapeDtypeStruct(s, t)...  72.5 us
    pallas_call x1, Pallas kernels, hand_out(): pl.pallas_call(hand_out_kernel, out_shape=tuple((jax.ShapeDtypeStruct(s,...  2.1 us

profile of v7, /device:TPU:1, one launch (start us, length us, event | category | flops | bytes accessed | tf_op | source)
XLA Modules:
  0.0 75.3 jit_solution(10069795064720645237)
XLA Ops:
  0.6 72.5 %layer_grads.1 = (bf16[1600,128]{1,0:T(8,128)(2,1)}, bf16[320,128]{1,0:T(8,128)(2,1)}, bf16[320,128]{1,0:T(8,128)(2,1)}, f32[5,2,16]{2,1,0:T(2,128)}, bf16[1600,...) custom-call(s32[25]{0:T(128)} %wins.1, bf16[5,64,128]{2,1,0:T(8,128)(2,1)} %bitcast.54, ...), custom_call_target="tpu_custom_call" | custom-call | tf_op jit(solution)/shard_map/layer_grads/pallas_call | solution.py:509
  73.2 2.1 %hand_out.1 = (bf16[1600,128]{1,0:T(8,128)(2,1)}, bf16[320,128]{1,0:T(8,128)(2,1)}, bf16[320,128]{1,0:T(8,128)(2,1)}, f32[5,2,16]{2,1,0:T(2,128)}, bf16[1600,128...) custom-call(bf16[1600,128]{1,0:T(8,128)(2,1)} %get-tuple-element.21.refs_0_, ...), custom_call_target="tpu_custom_call" | custom-call | tf_op jit(solution)/shard_map/hand_out/pallas_call | solution.py:554
